TPU v7x, 32 devices: a whole 2x2x4 slice. The times are simulated.
32 devices in a mesh: ia: 4 (over z), ja: 4 (over y, core), ka: 2 (over x).
Axes of the slice: x: 2, y: 2, z: 4, core: 2. Of those that a mesh axis runs over, the one named last changes fastest.
Arguments:
- features: bfloat16 [768, 6144], P('ia', ('ka', 'ja')), may hold values from -6 to 6
- in_weight: bfloat16 [6144, 24576], P(('ka', 'ia'), 'ja'), may hold values from -0.078125 to 0.078125
- out_weight: bfloat16 [24576, 6144], P(('ja', 'ia'), 'ka'), may hold values from -0.0390625 to 0.0390625
- cotangent: bfloat16 [768, 6144], P('ia', ('ka', 'ja')), may hold values from -1.5 to 1.5
Outputs:
- layer_out: bfloat16 [768, 6144], P('ia', ('ka', 'ja'))
- feature_grad: bfloat16 [768, 6144], P('ia', ('ka', 'ja'))
- in_weight_grad: bfloat16 [6144, 24576], P(('ka', 'ia'), 'ja')
- out_weight_grad: bfloat16 [24576, 6144], P(('ja', 'ia'), 'ka')
All inputs are finite; a program needn't handle non-finite values.
Results may differ from a plain program's by a relative error of at most 0.028.
Values may be sent and summed in bfloat16 or wider, within the bound.
No kernel may reach another device: no remote copies, remote signals or barrier semaphores. Data moves between devices by JAX's collectives and lax.ppermute only.
A program may use at most 192 MiB of HBM per device.

v0:
```python
import jax
import jax.numpy as jnp
from jax import lax
from jax.sharding import PartitionSpec as P

GELU_SCALE = 0.7978845608028654


def gelu_value(hidden):
    inner = GELU_SCALE * (hidden + 0.044715 * hidden * hidden * hidden)
    return 0.5 * hidden * (1.0 + jnp.tanh(inner))


def gelu_slope(hidden):
    tangent = jnp.tanh(GELU_SCALE * (hidden + 0.044715 * hidden * hidden * hidden))
    return 0.5 * (1.0 + tangent) + 0.5 * hidden * (1.0 - tangent * tangent) * GELU_SCALE * (
        1.0 + 3.0 * 0.044715 * hidden * hidden
    )


def transposed(left, right):
    return lax.dot_general(
        left, right, (((1,), (1,)), ((), ())), preferred_element_type=jnp.float32
    )


def inner_rows(left, right):
    return lax.dot_general(
        left, right, (((0,), (0,)), ((), ())), preferred_element_type=jnp.float32
    )


def local(features, in_weight, out_weight, cotangent):
    feature_block = lax.all_gather(features, "ja", axis=1, tiled=True)
    in_full = lax.all_gather(in_weight, "ia", axis=0, tiled=True)
    hidden_part = jnp.dot(feature_block, in_full, preferred_element_type=jnp.float32)
    pre_act = lax.psum_scatter(
        hidden_part.astype(jnp.bfloat16), "ka", scatter_dimension=1, tiled=True
    ).astype(jnp.float32)
    active_local = gelu_value(pre_act).astype(jnp.bfloat16)
    active_block = lax.all_gather(active_local, "ka", axis=1, tiled=True)
    out_full = lax.all_gather(out_weight, "ia", axis=0, tiled=True)
    output_part = jnp.dot(active_block, out_full, preferred_element_type=jnp.float32)
    layer_out = lax.psum_scatter(
        output_part.astype(jnp.bfloat16), "ja", scatter_dimension=1, tiled=True
    )
    cot_block = lax.all_gather(cotangent, "ja", axis=1, tiled=True)
    grad_part = transposed(cot_block, out_full)
    grad_active = lax.psum_scatter(
        grad_part.astype(jnp.bfloat16), "ka", scatter_dimension=1, tiled=True
    ).astype(jnp.float32)
    grad_local = (grad_active * gelu_slope(pre_act)).astype(jnp.bfloat16)
    grad_block = lax.all_gather(grad_local, "ka", axis=1, tiled=True)
    out_weight_grad = lax.psum_scatter(
        inner_rows(active_block, cot_block).astype(jnp.bfloat16),
        "ia",
        scatter_dimension=0,
        tiled=True,
    )
    in_weight_grad = lax.psum_scatter(
        inner_rows(feature_block, grad_block).astype(jnp.bfloat16),
        "ia",
        scatter_dimension=0,
        tiled=True,
    )
    input_part = transposed(grad_block, in_full)
    feature_grad = lax.psum_scatter(
        input_part.astype(jnp.bfloat16), "ja", scatter_dimension=1, tiled=True
    )
    return (layer_out, feature_grad, in_weight_grad, out_weight_grad)


def solution(mesh):
    placed = (
        P("ia", ("ka", "ja")),
        P(("ka", "ia"), "ja"),
        P(("ja", "ia"), "ka"),
        P("ia", ("ka", "ja")),
    )
    return jax.shard_map(
        local,
        mesh=mesh,
        in_specs=placed,
        out_specs=(
            P("ia", ("ka", "ja")),
            P("ia", ("ka", "ja")),
            P(("ka", "ia"), "ja"),
            P(("ja", "ia"), "ka"),
        ),
        check_vma=False,
    )
```

profile of v0, /device:TPU:4, one launch (start us, length us, event | category | flops | bytes accessed | tf_op | source)
XLA Modules:
  0.0 2774.2 jit_solution(2666115352377697138)
XLA Ops:
  7.2 0.7 all-gather.15.cloned.1.call-update
  7.9 0.7 all-gather.13.cloned.1.call-update
  8.7 0.7 all-gather.7.cloned.1.call-update
  9.4 0.5 all-gather.9.cloned.1.call-update
  10.0 17.1 all-gather.15.cloned.1.call-done
  27.1 634.2 %all-gather.13.cloned.1.call-done = bf16[6144,3072]{1,0:T(8,128)(2,1)} async-done(((bf16[1536,3072]{1,0:T(8,128)(2,1)}), bf16[6144,3072]{1,0:T(8,128)(2,1)}) %all-gather.13.cloned.1.call-update) | async-done | bytes 37748752 | tf_op jit(solution)/shard_map/all_gather | solution.py:42
  661.3 19.2 convolution_convert_fusion.1
  680.7 631.3 %all-gather.9.cloned.1.call-done = bf16[3072,6144]{1,0:T(8,128)(2,1)} async-done(((bf16[768,6144]{1,0:T(8,128)(2,1)}), bf16[3072,6144]{1,0:T(8,128)(2,1)}) %all-gather.9.cloned.1.call-update) | async-done | bytes 37748752 | tf_op jit(solution)/shard_map/all_gather | solution.py:35
  1311.9 18.1 convolution_convert_fusion.2
  1330.1 17.8 reduce-scatter.11.cloned.1.call-done
  1347.9 37.5 %reduce-scatter.7.cloned.1.call-done = bf16[192,3072]{1,0:T(8,128)(2,1)} async-done(((bf16[192,6144]{1,0:T(8,128)(2,1)}), bf16[192,3072]{1,0:T(8,128)(2,1)}) %reduce-scatter.7.cloned.1.call-update) | async-done | bytes 1179664 | tf_op jit(solution)/shard_map/reduce_scatter | solution.py:37
  1385.4 4.8 fusion.7
  1390.3 0.7 all-gather.11.cloned.1.call-update
  1391.2 35.2 %all-gather.17.cloned.1.call-done = bf16[192,6144]{1,0:T(8,128)(2,1)} async-done(((bf16[192,3072]{1,0:T(8,128)(2,1)}), bf16[192,6144]{1,0:T(8,128)(2,1)}) %all-gather.17.cloned.1.call-update) | async-done | bytes 2359312 | tf_op jit(solution)/shard_map/all_gather | solution.py:53
  1426.5 18.3 convert_bitcast_fusion
  1444.9 1.6 copy-done.1
  1446.5 18.9 convolution_convert_fusion.3
  1465.5 18.3 convolution_convert_fusion.4
  1484.1 16.1 convolution_convert_fusion
  1500.3 586.0 %reduce-scatter.15.cloned.1.call-done = bf16[768,6144]{0,1:T(8,128)(2,1)} async-done(((bf16[3072,6144]{0,1:T(8,128)(2,1)}), bf16[768,6144]{0,1:T(8,128)(2,1)}) %reduce-scatter.15.cloned.1.call-update) | async-done | bytes 9437200 | tf_op jit(solution)/shard_map/reduce_scatter | solution.py:60
  2086.3 12.6 copy.8
  2098.9 16.2 reduce-scatter.13.cloned.1.call-done
  2115.1 28.9 %reduce-scatter.9.cloned.1.call-done = bf16[192,768]{1,0:T(8,128)(2,1)} async-done(((bf16[192,3072]{1,0:T(8,128)(2,1)}), bf16[192,768]{1,0:T(8,128)(2,1)}) %reduce-scatter.9.cloned.1.call-update) | async-done | bytes 294928 | tf_op jit(solution)/shard_map/reduce_scatter | solution.py:44
  2144.0 623.3 %reduce-scatter.17.cloned.1.call-done = bf16[1536,3072]{1,0:T(8,128)(2,1)} async-done(((bf16[6144,3072]{1,0:T(8,128)(2,1)}), bf16[1536,3072]{1,0:T(8,128)(2,1)}) %reduce-scatter.17.cloned.1.call-update) | async-done | bytes 9437200 | tf_op jit(solution)/shard_map/reduce_scatter | solution.py:54
  (28 shorter events, 1.0 us)
Async XLA Ops:
  7.2 19.9 all-gather.15.cloned.1.call-start
  7.9 653.4 %all-gather.13.cloned.1.call-start = ((), (), s32[]{:S(2)}) async-start(), calls=%async_computation.10 | async-start | bytes 47185920 | tf_op jit(solution)/shard_map/all_gather | solution.py:42
  8.6 672.0 %all-gather.7.cloned.1.call-start = ((), (), s32[]{:S(2)}) async-start(), calls=%async_computation.6 | async-start | bytes 1474560 | tf_op jit(solution)/shard_map/all_gather | solution.py:34
  9.4 1302.5 %all-gather.9.cloned.1.call-start = ((), (), s32[]{:S(2)}) async-start(), calls=%async_computation.7 | async-start | bytes 47185920 | tf_op jit(solution)/shard_map/all_gather | solution.py:35
  10.0 1337.9 %reduce-scatter.11.cloned.1.call-start = ((), (), s32[]{:S(2)}) async-start(), calls=%async_computation.13 | async-start | bytes 3538944 | tf_op jit(solution)/shard_map/reduce_scatter | solution.py:49
  680.6 704.8 %reduce-scatter.7.cloned.1.call-start = ((), (), s32[]{:S(2)}) async-start(), calls=%async_computation.8 | async-start | bytes 3538944 | tf_op jit(solution)/shard_map/reduce_scatter | solution.py:37
  1330.1 96.4 %all-gather.17.cloned.1.call-start = ((), (), s32[]{:S(2)}) async-start(), calls=%async_computation.14 | async-start | bytes 3538944 | tf_op jit(solution)/shard_map/all_gather | solution.py:53
  1390.2 36.3 %copy-start.3 = (bf16[192,3072]{1,0:T(8,128)(2,1)S(1)}, bf16[192,3072]{1,0:T(8,128)(2,1)}, u32[]{:S(2)}) copy-start(bf16[192,3072]{1,0:T(8,128)(2,1)} %all-gather.7.cloned.1.call-done) | copy-start | bytes 3538948
  1390.3 75.2 %all-gather.11.cloned.1.call-start = ((), (), s32[]{:S(2)}) async-start(), calls=%async_computation.9 | async-start | bytes 3538944 | tf_op jit(solution)/shard_map/all_gather | solution.py:41
  1391.0 695.3 %reduce-scatter.15.cloned.1.call-start = ((), (), s32[]{:S(2)}) async-start(), calls=%async_computation.16 | async-start | bytes 47185920 | tf_op jit(solution)/shard_map/reduce_scatter | solution.py:60
  1444.8 1.7 copy-start.1
  1444.8 670.3 %reduce-scatter.13.cloned.1.call-start = ((), (), s32[]{:S(2)}) async-start(), calls=%async_computation.15 | async-start | bytes 1474560 | tf_op jit(solution)/shard_map/reduce_scatter | solution.py:67
  1465.4 18.7 copy-start.2
  1465.4 678.6 %reduce-scatter.9.cloned.1.call-start = ((), (), s32[]{:S(2)}) async-start(), calls=%async_computation.11 | async-start | bytes 1474560 | tf_op jit(solution)/shard_map/reduce_scatter | solution.py:44
  1465.5 18.7 copy-start
  1483.9 1283.5 %reduce-scatter.17.cloned.1.call-start = ((), (), s32[]{:S(2)}) async-start(), calls=%async_computation.17 | async-start | bytes 47185920 | tf_op jit(solution)/shard_map/reduce_scatter | solution.py:54
Sparse Core Ops, SparseCore 0:
  9.6 17.4 all-gather.14
  28.7 632.6 all-gather.12
  662.9 14.8 all-gather.6
  679.3 632.6 all-gather.8
  1314.6 33.2 reduce-scatter.10
  1350.7 34.6 reduce-scatter.6
  1390.4 36.0 all-gather.16
  1428.6 36.0 all-gather.10
  1467.1 619.1 reduce-scatter.14
  2089.5 25.6 reduce-scatter.12
  2118.3 25.7 reduce-scatter.8
  2146.9 620.3 reduce-scatter.16
where the time goes:
time: 2780 us; the launch traced here: 2770 us
  waiting for transfers between devices  2630 us (95%)
  matrix products  109 us (4%)
    all_gather x1, waiting for transfers between devices, local(): out_full = lax.all_gather(out_weight, 'ia', axis=0, tiled=True)  634 us
    all_gather x1, waiting for transfers between devices, local(): in_full = lax.all_gather(in_weight, 'ia', axis=0, tiled=True)  631 us
    reduce_scatter x1, waiting for transfers between devices, local(): lax.psum_scatter(inner_rows(active_block, cot_block).astype(jnp.bfloat16)...  623 us
    reduce_scatter x1, waiting for transfers between devices, local(): lax.psum_scatter(inner_rows(feature_block, grad_block).astype(jnp.bfloat1...  586 us
  transfers between devices with their start and end apart: 12, of which 10 were waited for; matrix products, arithmetic and copies ran while one was open for 4% of the time, Pallas kernels for 0%

commit v1 on v0

v1 whole, which is shorter than its diff:
```python
import functools

import jax
import jax.numpy as jnp
from jax import lax
from jax.experimental import pallas as pl
from jax.experimental.pallas import tpu as pltpu
from jax.sharding import PartitionSpec as P

GELU_SCALE = 0.7978845608028654
VMEM_BYTES = 48 * 1024 * 1024


def gelu_value(hidden):
    inner = GELU_SCALE * (hidden + 0.044715 * hidden * hidden * hidden)
    return 0.5 * hidden * (1.0 + jnp.tanh(inner))


def gelu_slope(hidden):
    tangent = jnp.tanh(GELU_SCALE * (hidden + 0.044715 * hidden * hidden * hidden))
    return 0.5 * (1.0 + tangent) + 0.5 * hidden * (1.0 - tangent * tangent) * GELU_SCALE * (
        1.0 + 3.0 * 0.044715 * hidden * hidden
    )


def transposed(left, right):
    return lax.dot_general(
        left, right, (((1,), (1,)), ((), ())), preferred_element_type=jnp.float32
    )


def inner_rows(left, right):
    return lax.dot_general(
        left, right, (((0,), (0,)), ((), ())), preferred_element_type=jnp.float32
    )


def flip(block, axis, size, bit):
    return lax.ppermute(block, axis, [(d, d ^ bit) for d in range(size)])


def reversed_bits(size):
    order = [0]
    bit = size // 2
    while bit:
        order = [o for o in order] + [o + bit for o in order]
        bit //= 2
    return order


def column_tile(width):
    for tile in (768, 512, 384, 256, 128):
        if width % tile == 0:
            return tile
    return width


def nothing(block, *refs):
    del block, refs


def after(block, *earlier):
    return pl.pallas_call(
        nothing,
        out_shape=jax.ShapeDtypeStruct(block.shape, block.dtype),
        in_specs=[pl.BlockSpec(memory_space=pl.ANY)] * (1 + len(earlier)),
        out_specs=pl.BlockSpec(memory_space=pl.ANY),
        input_output_aliases={0: 0},
        cost_estimate=pl.CostEstimate(flops=0, bytes_accessed=0, transcendentals=0),
    )(block, *earlier)


def up_kernel(order, rows, weight, keep, send):
    del order
    part = jnp.dot(rows[...], weight[...], preferred_element_type=jnp.float32)
    half = part.shape[0] // 2
    keep[...] = part[:half].reshape(keep.shape)
    send[...] = part[half:].reshape(send.shape).astype(send.dtype)


def up_parts(order, rows, weight, halves, count, blocks):
    depth, width = weight.shape
    span = width // blocks
    tile = column_tile(span)
    tiles = span // tile
    shape = (halves, blocks, count, span)
    place = pl.BlockSpec((halves, None, count, tile), lambda b, n, order: (0, b, 0, n))
    return pl.pallas_call(
        up_kernel,
        grid_spec=pltpu.PrefetchScalarGridSpec(
            num_scalar_prefetch=1,
            grid=(blocks, tiles),
            in_specs=[
                pl.BlockSpec(rows.shape, lambda b, n, order: (0, 0)),
                pl.BlockSpec((depth, tile), lambda b, n, order: (0, order[b] * tiles + n)),
            ],
            out_specs=[place, place],
        ),
        out_shape=[
            jax.ShapeDtypeStruct(shape, jnp.float32),
            jax.ShapeDtypeStruct(shape, jnp.bfloat16),
        ],
        compiler_params=pltpu.CompilerParams(vmem_limit_bytes=VMEM_BYTES),
        cost_estimate=pl.CostEstimate(
            flops=2 * rows.shape[0] * depth * width,
            bytes_accessed=2 * depth * width + 6 * halves * count * width,
            transcendentals=0,
        ),
    )(order, rows, weight)


def block_kernel(order, rows, weight, out):
    del order
    part = jnp.dot(rows[...], weight[...], preferred_element_type=jnp.float32)
    out[...] = part.astype(out.dtype)


def up_blocks(order, rows, weight, blocks, kind):
    depth, width = weight.shape
    span = width // blocks
    tile = column_tile(span)
    tiles = span // tile
    chosen, count = order.shape[0], rows.shape[0]
    return pl.pallas_call(
        block_kernel,
        grid_spec=pltpu.PrefetchScalarGridSpec(
            num_scalar_prefetch=1,
            grid=(chosen, tiles),
            in_specs=[
                pl.BlockSpec(rows.shape, lambda b, n, order: (0, 0)),
                pl.BlockSpec((depth, tile), lambda b, n, order: (0, order[b] * tiles + n)),
            ],
            out_specs=pl.BlockSpec((None, count, tile), lambda b, n, order: (b, 0, n)),
        ),
        out_shape=jax.ShapeDtypeStruct((chosen, count, span), kind),
        compiler_params=pltpu.CompilerParams(vmem_limit_bytes=VMEM_BYTES),
        cost_estimate=pl.CostEstimate(
            flops=2 * count * depth * span * chosen,
            bytes_accessed=2 * chosen * span * (depth + 2 * count),
            transcendentals=0,
        ),
    )(order, rows, weight)


def down_kernel(order, rows, weight, keep, send, total):
    del order
    step = pl.program_id(1)
    part = transposed(rows[...], weight[...])

    @pl.when(step == 0)
    def _():
        total[...] = part

    @pl.when(step > 0)
    def _():
        total[...] += part

    @pl.when(step == pl.num_programs(1) - 1)
    def _():
        half = total.shape[0] // 2
        keep[...] = total[:half].reshape(keep.shape)
        send[...] = total[half:].reshape(send.shape).astype(send.dtype)


def down_parts(order, rows, weight, parts):
    blocks, tokens, span = rows.shape
    width = weight.shape[0]
    tile = next(t for t in (512, 384, 256, 128) if width % t == 0)
    shape = (parts // 2, tokens // parts, width)
    place = pl.BlockSpec(shape[:2] + (tile,), lambda n, b, order: (0, 0, n))
    return pl.pallas_call(
        down_kernel,
        grid_spec=pltpu.PrefetchScalarGridSpec(
            num_scalar_prefetch=1,
            grid=(width // tile, blocks),
            in_specs=[
                pl.BlockSpec((None, tokens, span), lambda n, b, order: (b, 0, 0)),
                pl.BlockSpec((tile, span), lambda n, b, order: (n, order[b])),
            ],
            out_specs=[place, place],
            scratch_shapes=[pltpu.VMEM((tokens, tile), jnp.float32)],
        ),
        out_shape=[
            jax.ShapeDtypeStruct(shape, jnp.float32),
            jax.ShapeDtypeStruct(shape, jnp.bfloat16),
        ],
        compiler_params=pltpu.CompilerParams(vmem_limit_bytes=VMEM_BYTES),
        cost_estimate=pl.CostEstimate(
            flops=2 * tokens * width * blocks * span,
            bytes_accessed=2 * blocks * span * (width + 3 * tokens) + 3 * tokens * width,
            transcendentals=0,
        ),
    )(order, rows, weight)


def active_kernel(keep, got, active):
    pre = keep[...] + got[...].astype(jnp.float32)
    active[...] = gelu_value(pre).astype(active.dtype)


def slope_kernel(keep, got, grad_keep, grad_got, grad):
    pre = keep[...] + got[...].astype(jnp.float32)
    above = grad_keep[...] + grad_got[...].astype(jnp.float32)
    grad[...] = (above * gelu_slope(pre)).astype(grad.dtype)


def on_chunk(kernel, arrays, place):
    count, span = arrays[0].shape
    tile = column_tile(span)
    here = pl.BlockSpec((count, tile), lambda n: (0, n))
    there = pl.BlockSpec((count, tile), lambda n: (place, n))
    return pl.pallas_call(
        kernel,
        grid=(span // tile,),
        in_specs=[here, here] + [there] * (len(arrays) - 2),
        out_specs=here,
        out_shape=jax.ShapeDtypeStruct((count, span), jnp.bfloat16),
        compiler_params=pltpu.CompilerParams(vmem_limit_bytes=VMEM_BYTES),
        cost_estimate=pl.CostEstimate(
            flops=20 * count * span,
            bytes_accessed=8 * count * span,
            transcendentals=count * span,
        ),
    )(*arrays)


def input_kernel(order, weight, *refs):
    del order
    pieces, out, total, stack = refs[:-3], refs[-3], refs[-2], refs[-1]
    first = (pl.program_id(0) == 0) & (pl.program_id(1) == 0)
    last = (pl.program_id(0) == pl.num_programs(0) - 1) & (
        pl.program_id(1) == pl.num_programs(1) - 1
    )

    @pl.when(first)
    def _():
        total[...] = jnp.zeros_like(total)

    row = 0
    for piece in pieces:
        for part in range(piece.shape[0]):
            stack[pl.ds(row, piece.shape[1]), :] = piece[part]
            row += piece.shape[1]
    total[...] += transposed(stack[...], weight[...])

    @pl.when(last)
    def _():
        out[...] = total[...].astype(out.dtype)


def input_parts(order, pieces, weight, blocks):
    depth, width = weight.shape
    span = width // blocks
    tile = column_tile(span)
    tiles = span // tile
    rows = sum(piece.shape[0] * piece.shape[2] for piece in pieces)
    return pl.pallas_call(
        input_kernel,
        grid_spec=pltpu.PrefetchScalarGridSpec(
            num_scalar_prefetch=1,
            grid=(blocks, tiles),
            in_specs=[
                pl.BlockSpec((depth, tile), lambda b, n, order: (0, order[b] * tiles + n))
            ]
            + [
                pl.BlockSpec(
                    (piece.shape[0], None, piece.shape[2], tile), lambda b, n, order: (0, b, 0, n)
                )
                for piece in pieces
            ],
            out_specs=pl.BlockSpec((rows, depth), lambda b, n, order: (0, 0)),
            scratch_shapes=[
                pltpu.VMEM((rows, depth), jnp.float32),
                pltpu.VMEM((rows, tile), jnp.bfloat16),
            ],
        ),
        out_shape=jax.ShapeDtypeStruct((rows, depth), jnp.bfloat16),
        compiler_params=pltpu.CompilerParams(vmem_limit_bytes=VMEM_BYTES),
        cost_estimate=pl.CostEstimate(
            flops=2 * rows * depth * width,
            bytes_accessed=2 * depth * width + 2 * rows * (depth + width),
            transcendentals=0,
        ),
    )(order, weight, *pieces)


def weight_kernel(order, columns, *refs):
    del order
    pieces, out, stack = refs[:-2], refs[-2], refs[-1]
    row = 0
    for piece in pieces:
        for part in range(piece.shape[0]):
            stack[pl.ds(row, piece.shape[1]), :] = piece[part]
            row += piece.shape[1]
    out[...] = jnp.dot(
        columns[...], stack[...], preferred_element_type=jnp.float32
    ).astype(out.dtype)


def weight_parts(order, columns, pieces, blocks):
    depth, rows = columns.shape
    span = pieces[0].shape[3]
    tile = column_tile(span)
    tiles = span // tile
    width = span * blocks
    return pl.pallas_call(
        weight_kernel,
        grid_spec=pltpu.PrefetchScalarGridSpec(
            num_scalar_prefetch=1,
            grid=(blocks, tiles),
            in_specs=[pl.BlockSpec((depth, rows), lambda b, n, order: (0, 0))]
            + [
                pl.BlockSpec(
                    (piece.shape[0], None, piece.shape[2], tile), lambda b, n, order: (0, b, 0, n)
                )
                for piece in pieces
            ],
            out_specs=pl.BlockSpec(
                (depth, tile), lambda b, n, order: (0, order[b] * tiles + n)
            ),
            scratch_shapes=[pltpu.VMEM((rows, tile), jnp.bfloat16)],
        ),
        out_shape=jax.ShapeDtypeStruct((depth, width), jnp.bfloat16),
        compiler_params=pltpu.CompilerParams(vmem_limit_bytes=VMEM_BYTES),
        cost_estimate=pl.CostEstimate(
            flops=2 * rows * depth * width,
            bytes_accessed=2 * rows * (depth + width) + 2 * depth * width,
            transcendentals=0,
        ),
    )(order, columns, *pieces)


def relative(parts, own):
    return jnp.stack(
        [
            lax.dynamic_index_in_dim(parts, own ^ s, 0, keepdims=False)
            for s in range(parts.shape[0])
        ]
    )


def halved(keep, send, axis, size, bit, down):
    while True:
        got = flip(send, axis, size, bit)
        if keep.shape[0] == 1:
            return keep[0], got[0]
        total = keep + got.astype(jnp.float32)
        half = total.shape[0] // 2
        keep, send = total[:half], total[half:].astype(jnp.bfloat16)
        bit = bit // 2 if down else bit * 2


def doubled(block, axis, size, up=False):
    bits = [1 << b for b in range(size.bit_length() - 1)]
    for bit in bits if up else bits[::-1]:
        block = jnp.concatenate([block, flip(block, axis, size, bit)], axis=0)
    return block


def natural(parts):
    return jnp.stack([parts[s] for s in reversed_bits(parts.shape[0])])


def local(ni, nj, nk, features, in_weight, out_weight, cotangent):
    tokens = features.shape[0] * ni
    depth = in_weight.shape[0]
    share = tokens // nk
    chunks = next(c for c in (4, 2, 1) if share % (16 * c) == 0)
    count = share // chunks
    own_i = lax.axis_index("ia")
    own_j = lax.axis_index("ja")
    own_k = lax.axis_index("ka")
    order = own_i ^ jnp.array(reversed_bits(ni), jnp.int32)
    swap = [(a * nj + b, b * ni + a) for a in range(ni) for b in range(nj)]
    crosswise = [chunk == 1 for chunk in range(chunks)]

    if ni == nj:
        turned = lax.ppermute(features, ("ia", "ja"), swap)
        feature_cols = lax.all_gather(turned, "ja", axis=0, tiled=True)
    else:
        feature_rows = lax.all_gather(features, "ja", axis=1, tiled=True)
        feature_cols = lax.all_to_all(
            feature_rows, "ia", split_axis=1, concat_axis=0, tiled=True
        )
    shuffled = relative(feature_cols.reshape(nk, share, depth), own_k)
    shuffled = shuffled.reshape(nk, chunks, count, depth).transpose(1, 0, 2, 3)
    shuffled = shuffled.reshape(tokens, depth)

    half = ni // 2
    straight = [chunk for chunk in range(chunks) if not crosswise[chunk]]
    across = [chunk for chunk in range(chunks) if crosswise[chunk]]
    rows_of = [shuffled[c * nk * count : (c + 1) * nk * count] for c in range(chunks)]
    kept = {}
    for chunk in straight:
        rows = rows_of[chunk]
        if chunk != straight[0]:
            rows = after(rows, kept[straight[0]][1])
        kept[chunk] = up_parts(order, rows, in_weight, nk // 2, count, ni)
    totals = {}
    for chunk in across:
        rows = after(rows_of[chunk], kept[straight[0]][1])
        send = up_blocks(order[half:], rows, in_weight, ni, jnp.bfloat16)
        keep = up_blocks(order[:half], rows, in_weight, ni, jnp.float32)
        keep, got = halved(keep, send, "ia", ni, 1, False)
        totals[chunk] = (keep + got.astype(jnp.float32)).reshape(nk, count, -1)

    if ni == nj:
        cotangent = after(cotangent, turned)
    cot_tokens = relative(natural(doubled(cotangent[None], "ia", ni)), own_i)
    cot_tokens = relative(cot_tokens.reshape(nk, share, -1), own_k)
    cot_tokens = after(cot_tokens.reshape(1, tokens, -1), kept[straight[0]][1])
    cot_parts = doubled(cot_tokens, "ja", nj)
    cot_order = own_j ^ jnp.array(reversed_bits(nj), jnp.int32)
    if cot_parts.shape[-1] % 128:
        cot_parts = relative(natural(cot_parts), own_j).transpose(1, 0, 2)
        cot_parts = cot_parts.reshape(1, tokens, -1)
        cot_order = jnp.zeros((1,), jnp.int32)
    grad_keep, grad_send = down_parts(cot_order, cot_parts, out_weight, nk)

    sums = [None] * chunks
    came = None
    for chunk in straight + across:
        if crosswise[chunk]:
            total = totals[chunk]
            send = after(total[nk // 2 :].astype(jnp.bfloat16), came)
            sums[chunk] = halved(total[: nk // 2], send, "ka", nk, nk // 2, True)
            came = sums[chunk][1]
        else:
            keep, send = kept[chunk]
            send = send if came is None else after(send, came)
            keep, came = halved(keep, send, "ka", nk, nk // 2, True)
            total = keep + came.astype(jnp.float32)
            sums[chunk] = halved(
                total[:half], total[half:].astype(jnp.bfloat16), "ia", ni, 1, False
            )
    grad_keep, grad_got = halved(
        grad_keep, after(grad_send, came), "ka", nk, nk // 2, True
    )
    actives = [on_chunk(active_kernel, sums[chunk], 0) for chunk in range(chunks)]
    parts = after(jnp.concatenate(actives, axis=0), grad_got)[None]
    active_rows = doubled(parts, "ka", nk, True).reshape(tokens, -1)
    came = active_rows

    firsts = {}
    for chunk in straight + across:
        arrays = list(sums[chunk]) + [grad_keep, grad_got]
        block = on_chunk(slope_kernel, arrays, chunk)[None]
        if crosswise[chunk]:
            block = doubled(block, "ka", nk, True).reshape(1, nk * count, -1)
        bit = ni // 2
        firsts[chunk] = jnp.concatenate([block, flip(block, "ia", ni, bit)], axis=0)
    turned_blocks = {}
    for chunk in straight + across:
        block = firsts[chunk]
        bit = ni // 4
        while bit:
            block = jnp.concatenate([block, flip(block, "ia", ni, bit)], axis=0)
            bit //= 2
        turned_blocks[chunk] = block

    columns = active_rows.T
    out_weight_grad = weight_parts(
        cot_order, columns, [cot_parts[None]], cot_parts.shape[0]
    )
    pieces_of = {}
    input_rows = [None] * chunks
    for place, chunk in enumerate(straight):
        earlier = [came]
        if place + 1 < len(straight):
            earlier.append(firsts[straight[place + 1]])
        if place == 0:
            gate = earlier[-1]
        if place == 2:
            earlier += [input_rows[straight[0]], out_weight_grad]
        block = after(turned_blocks[chunk][None], *earlier)
        pieces = [block]
        bit = 1
        while bit < nk:
            came = flip(block, "ka", nk, bit)
            pieces.append(came)
            bit *= 2
            if bit < nk:
                block = jnp.concatenate([block, came], axis=0)
        pieces_of[chunk] = pieces
        if place == len(straight) - 1:
            for other in across:
                block = turned_blocks[other]
                pieces_of[other] = [block.reshape(1, ni, nk * count, -1)]
                input_rows[other] = input_parts(order, pieces_of[other], in_weight, ni)
            done = [rows for rows in input_rows if rows is not None]
            if done:
                pieces = [after(pieces[0], *done)] + pieces[1:]
        input_rows[chunk] = input_parts(order, pieces, in_weight, ni)
    input_rows = [rows.reshape(nk, count, depth) for rows in input_rows]
    in_weight_grad = weight_parts(
        order,
        shuffled.T,
        [piece for chunk in range(chunks) for piece in pieces_of[chunk]],
        ni,
    )

    input_part = jnp.stack(input_rows, axis=1).reshape(nk, share, depth)
    input_part = relative(input_part, own_k).reshape(tokens, depth)
    if ni == nj:
        parts = natural(relative(input_part.reshape(nj, tokens // nj, depth), own_j))
        keep, got = halved(parts[: nj // 2], parts[nj // 2 :], "ja", nj, 1, False)
        input_sum = (keep + got.astype(jnp.float32)).astype(jnp.bfloat16)
        feature_grad = lax.ppermute(input_sum, ("ia", "ja"), swap)
    else:
        input_full = lax.all_to_all(
            input_part, "ia", split_axis=0, concat_axis=1, tiled=True
        )
        feature_grad = lax.psum_scatter(
            input_full, "ja", scatter_dimension=1, tiled=True
        )

    active_rows = after(active_rows, gate)
    output_part = jnp.dot(active_rows, out_weight, preferred_element_type=jnp.float32)
    output_cols = lax.psum_scatter(
        output_part.astype(jnp.bfloat16), "ja", scatter_dimension=1, tiled=True
    )
    output_cols = relative(output_cols.reshape(nk, share, -1), own_k)
    layer_out = lax.psum_scatter(
        output_cols.reshape(tokens, -1), "ia", scatter_dimension=0, tiled=True
    )
    return (layer_out, feature_grad, in_weight_grad, out_weight_grad)


def solution(mesh):
    placed = (
        P("ia", ("ka", "ja")),
        P(("ka", "ia"), "ja"),
        P(("ja", "ia"), "ka"),
        P("ia", ("ka", "ja")),
    )
    return jax.shard_map(
        functools.partial(local, *(mesh.shape[axis] for axis in ("ia", "ja", "ka"))),
        mesh=mesh,
        in_specs=placed,
        out_specs=(
            P("ia", ("ka", "ja")),
            P("ia", ("ka", "ja")),
            P(("ka", "ia"), "ja"),
            P(("ja", "ia"), "ka"),
        ),
        check_vma=False,
    )
```

time: 2780 us -> 461 us (0.17)
  waiting for transfers between devices: 2630 us -> 191 us
  Pallas kernels: 0 us -> 121 us
  matrix products: 109 us -> 12.3 us
  starting transfers between devices: 0.88 us -> 44.4 us
  other arithmetic: 4.81 us -> 35.1 us
    all_gather x6 -> x1, waiting for transfers between devices: 1320 us -> 2.1 us  [local(): feature_cols = lax.all_gather(turned, 'ja', axis=0, tiled=True)]
    reduce_scatter x5 -> x1, waiting for transfers between devices: 1280 us -> 0.01 us  [local(): lax.psum_scatter(output_cols.reshape(tokens, -1), 'ia', scatter_dimension...]
    ppermute x0 -> x34, waiting for transfers between devices: none -> 189 us  [the longest x32 149 us: flip(): return lax.ppermute(block, axis, [(d, d ^ bit) for d in range(size)])]
    pallas_call x0 -> x35, Pallas kernels: none -> 121 us  [the longest x4 36.5 us: input_parts(): pl.pallas_call(input_kernel, grid_spec=pltpu.PrefetchScalarGridSpec(num_s...]
    dot_general x6 -> x1, matrix products: 109 us -> 12.3 us  [local(): jnp.dot(active_rows, out_weight, preferred_element_type=jnp.float32)]
    ppermute x0 -> x34, starting transfers between devices: none -> 44.2 us  [the longest x32 34.5 us: flip(): return lax.ppermute(block, axis, [(d, d ^ bit) for d in range(size)])]
    reduce_scatter x1, waiting for transfers between devices: 28.9 us -> 0.02 us  [local(): lax.psum_scatter(output_part.astype(jnp.bfloat16), 'ja', scatter_dimensio...]
  transfers between devices with their start and end apart: 12 -> 37, of which waited for: 10 -> 18; matrix products, arithmetic and copies ran while one was open for 4% -> 10% of each run, Pallas kernels for 0% -> 26%
where the time goes in v1:
time: 461 us; the launch traced here: 459 us
  waiting for transfers between devices  191 us (41%)
  Pallas kernels  121 us (26%)
  starting transfers between devices  44.4 us (10%)
  local copies, waits for them, and re-layouts  40.2 us (9%)
  other arithmetic  35.1 us (8%)
  between operations  14.8 us (3%)
  matrix products  12.3 us (3%)
    ppermute x32, waiting for transfers between devices, flip(): return lax.ppermute(block, axis, [(d, d ^ bit) for d in range(size)])  149 us
    pallas_call x4, Pallas kernels, input_parts(): pl.pallas_call(input_kernel, grid_spec=pltpu.PrefetchScalarGridSpec(num_s...  36.5 us
    ppermute x32, starting transfers between devices, flip(): return lax.ppermute(block, axis, [(d, d ^ bit) for d in range(size)])  34.5 us
    ppermute x1, waiting for transfers between devices, local(): feature_grad = lax.ppermute(input_sum, ('ia', 'ja'), swap)  24.9 us
    pallas_call x3, Pallas kernels, up_parts(): pl.pallas_call(up_kernel, grid_spec=pltpu.PrefetchScalarGridSpec(num_scal...  24.5 us
    pallas_call x2, Pallas kernels, weight_parts(): pl.pallas_call(weight_kernel, grid_spec=pltpu.PrefetchScalarGridSpec(num_...  24.4 us
    unnamed x136, local copies, waits for them, and re-layouts  23 us
    pallas_call x1, Pallas kernels, down_parts(): pl.pallas_call(down_kernel, grid_spec=pltpu.PrefetchScalarGridSpec(num_sc...  17 us
  transfers between devices with their start and end apart: 37, of which 18 were waited for; matrix products, arithmetic and copies ran while one was open for 10% of the time, Pallas kernels for 26%

profile of v1, /device:TPU:4, one launch (start us, length us, event | category | flops | bytes accessed | tf_op | source)
XLA Modules:
  0.0 458.5 jit_solution(911068524462084343)
XLA Ops:
  13.4 15.2 %collective-permute-done.refs_0_ = bf16[192,768]{1,0:T(8,128)(2,1)S(1)} collective-permute-done((bf16[192,768]{1,0:T(8,128)(2,1)}, bf16[192,768]{1,0:T(8,128)(2,1)S(1)}, u32[]{:S(2)}, u32[]{:S(2)}) %collective-permute-start) | collective-permute-done | bytes 294944 | tf_op jit(solution)/shard_map/ppermute | solution.py:378
  29.6 14.0 %collective-permute-done.13 = bf16[1,192,768]{2,1,0:T(8,128)(2,1)S(1)} collective-permute-done((bf16[1,192,768]{2,1,0:T(8,128)(2,1)}, bf16[1,192,768]{2,1,0:T(8,128)(2,1)S(1)}, u32[]{:S(2)}, u32[]{:S(2)}) %collective-permute-start.13) | collective-permute-done | bytes 294944 | tf_op jit(solution)/shard_map/ppermute | solution.py:39
  50.3 8.2 %shard_map.93 = (f32[1,4,96,1536]{3,2,1,0:T(8,128)S(1)}, bf16[1,4,96,1536]{3,2,1,0:T(8,128)(2,1)S(1)}) custom-call(s32[4]{0:T(128)S(1)} %get-tuple-element.45.order, bf16[192,768]{1,0:T(8,128)(2,1)S(1)} %bitcast.99, bf16[768,6144]{1,0:T(8,128)(2,1)} %weight.19), custom_call_target="tpu_custom_call" | custom-call | flops 1811939328 | bytes 12976128 | tf_op jit(solution)/shard_map/pallas_call | solution.py:88
  62.6 5.5 %shard_map.97 = bf16[2,192,1536]{2,1,0:T(8,128)(2,1)} custom-call(s32[2]{0:T(128)S(1)} %get-tuple-element.46.order, bf16[192,768]{1,0:T(8,128)(2,1)S(1)} %copy-done.17, bf16[768,6144]{1,0:T(8,128)(2,1)} %weight.19), custom_call_target="tpu_custom_call" | custom-call | flops 905969664 | bytes 7077888 | tf_op jit(solution)/shard_map/pallas_call | solution.py:124
  79.4 8.2 %shard_map.101 = (f32[1,4,96,1536]{3,2,1,0:T(8,128)S(1)}, bf16[1,4,96,1536]{3,2,1,0:T(8,128)(2,1)S(1)}) custom-call(s32[4]{0:T(128)S(1)} %get-tuple-element.45.order, bf16[192,768]{1,0:T(8,128)(2,1)S(1)} %copy-done.24, bf16[768,6144]{1,0:T(8,128)(2,1)} %weight.19), custom_call_target="tpu_custom_call" | custom-call | flops 1811939328 | bytes 12976128 | tf_op jit(solution)/shard_map/pallas_call | solution.py:88
  90.0 8.2 %shard_map.99 = (f32[1,4,96,1536]{3,2,1,0:T(8,128)S(1)}, bf16[1,4,96,1536]{3,2,1,0:T(8,128)(2,1)S(1)}) custom-call(s32[4]{0:T(128)S(1)} %get-tuple-element.45.order, bf16[192,768]{1,0:T(8,128)(2,1)S(1)} %copy-done.23, bf16[768,6144]{1,0:T(8,128)(2,1)} %weight.19), custom_call_target="tpu_custom_call" | custom-call | flops 1811939328 | bytes 12976128 | tf_op jit(solution)/shard_map/pallas_call | solution.py:88
  111.7 20.1 %collective-permute-done.5 = bf16[1,192,1536]{2,1,0:T(8,128)(2,1)S(1)} collective-permute-done((bf16[1,192,1536]{2,1,0:T(8,128)(2,1)S(1)}, bf16[1,192,1536]{2,1,0:T(8,128)(2,1)S(1)}, u32[]{:S(2)}, u32[]{:S(2)}) %collective-permute-start.5) | collective-permute-done | bytes 589856 | tf_op jit(solution)/shard_map/ppermute | solution.py:39
  140.0 14.5 %collective-permute-done.3 = bf16[1,96,1536]{2,1,0:T(8,128)(2,1)S(1)} collective-permute-done((bf16[1,96,1536]{2,1,0:T(8,128)(2,1)S(1)}, bf16[1,96,1536]{2,1,0:T(8,128)(2,1)S(1)}, u32[]{:S(2)}, u32[]{:S(2)}) %collective-permute-start.3) | collective-permute-done | bytes 294944 | tf_op jit(solution)/shard_map/ppermute | solution.py:39
  160.6 5.6 %fusion.2 = (bf16[1,4,768,768]{3,2,1,0:T(8,128)(2,1)}, bf16[4,768,768]{2,1,0:T(8,128)(2,1)}) fusion(bf16[2,768,768]{2,1,0:T(8,128)(2,1)} %collective-permute-done.16, bf16[1,768,768]{2,1,0:T(8,128)(2,1)} %collective-permute-done.15, bf16[1,768,768]{2,1,0:T(8,128)(2,1)S(1)} %copy-done.48), kind=kLoop, calls=%fused_computation.66 | loop fusion | flops 4718592 | bytes 14155776 | tf_op jit(solution)/shard_map/broadcast_in_dim | solution.py:463
  170.3 17.0 %shard_map.110 = (f32[1,384,1536]{2,1,0:T(8,128)S(1)}, bf16[1,384,1536]{2,1,0:T(8,128)(2,1)S(1)}) custom-call(s32[4]{0:T(128)S(1)} %get-tuple-element.44.order, bf16[4,768,768]{2,1,0:T(8,128)(2,1)} %get-tuple-element.21.rows, bf16[1536,3072]{1,0:T(8,128)(2,1)} %weight.15), custom_call_target="tpu_custom_call" | custom-call | flops 7247757312 | bytes 27131904 | tf_op jit(solution)/shard_map/pallas_call | solution.py:171
  196.5 11.6 %collective-permute-done.12 = bf16[1,96,1536]{2,1,0:T(8,128)(2,1)S(1)} collective-permute-done((bf16[1,96,1536]{2,1,0:T(8,128)(2,1)S(1)}, bf16[1,96,1536]{2,1,0:T(8,128)(2,1)S(1)}, u32[]{:S(2)}, u32[]{:S(2)}) %collective-permute-start.12) | collective-permute-done | bytes 294944 | tf_op jit(solution)/shard_map/ppermute | solution.py:39
  219.3 8.9 %collective-permute-done.20 = bf16[1,96,1536]{2,1,0:T(8,128)(2,1)} collective-permute-done((bf16[1,96,1536]{2,1,0:T(8,128)(2,1)}, bf16[1,96,1536]{2,1,0:T(8,128)(2,1)}, u32[]{:S(2)}, u32[]{:S(2)}) %collective-permute-start.20) | collective-permute-done | bytes 294944 | tf_op jit(solution)/shard_map/ppermute | solution.py:39
  234.6 12.8 %collective-permute-done.19 = bf16[1,96,1536]{2,1,0:T(8,128)(2,1)S(1)} collective-permute-done((bf16[1,96,1536]{2,1,0:T(8,128)(2,1)S(1)}, bf16[1,96,1536]{2,1,0:T(8,128)(2,1)S(1)}, u32[]{:S(2)}, u32[]{:S(2)}) %collective-permute-start.19) | collective-permute-done | bytes 294944 | tf_op jit(solution)/shard_map/ppermute | solution.py:39
  257.7 12.3 %convolution_convert_fusion = bf16[768,3072]{1,0:T(8,128)(2,1)} fusion(bf16[768,1536]{1,0:T(8,128)(2,1)} %shard_map.114, bf16[1536,3072]{1,0:T(8,128)(2,1)} %weight.15), kind=kOutput, calls=%fused_computation | convolution fusion | flops 7250116608 | bytes 16515072 | tf_op jit(solution)/shard_map/dot_general | solution.py:518
  278.5 23.8 %collective-permute-done.23 = bf16[1,96,1536]{2,1,0:T(8,128)(2,1)S(1)} collective-permute-done((bf16[1,96,1536]{2,1,0:T(8,128)(2,1)S(1)}, bf16[1,96,1536]{2,1,0:T(8,128)(2,1)S(1)}, u32[]{:S(2)}, u32[]{:S(2)}) %collective-permute-start.23) | collective-permute-done | bytes 294944 | tf_op jit(solution)/shard_map/ppermute | solution.py:39
  308.4 20.6 %collective-permute-done.24 = bf16[1,192,1536]{2,1,0:T(8,128)(2,1)S(1)} collective-permute-done((bf16[1,192,1536]{2,1,0:T(8,128)(2,1)S(1)}, bf16[1,192,1536]{2,1,0:T(8,128)(2,1)S(1)}, u32[]{:S(2)}, u32[]{:S(2)}) %collective-permute-start.24) | collective-permute-done | bytes 589856 | tf_op jit(solution)/shard_map/ppermute | solution.py:39
  332.6 11.4 %shard_map.123.refs_2_ = bf16[1536,3072]{1,0:T(8,128)(2,1)} custom-call(s32[4]{0:T(128)S(1)} %get-tuple-element.44.order, bf16[1536,768]{1,0:T(8,128)(2,1)S(1)} %bitcast.98, bf16[1,4,768,768]{3,2,1,0:T(8,128)(2,1)} %get-tuple-element.20.refs_0_), custom_call_target="tpu_custom_call" | custom-call | flops 7247757312 | bytes 16515072 | tf_op jit(solution)/shard_map/pallas_call | solution.py:306
  344.0 8.9 %shard_map.117.refs_1_.refs_0_ = bf16[192,768]{1,0:T(8,128)(2,1)S(1)} custom-call(s32[4]{0:T(128)S(1)} %get-tuple-element.45.order, bf16[768,6144]{1,0:T(8,128)(2,1)} %weight.19, bf16[1,4,96,1536]{3,2,1,0:T(8,128)(2,1)S(1)} %copy-done.4, bf16[1,4,96,1536]{3,2,1,0:T(8,128)(2,1)} %collective-permute-done.22.refs_1_.refs_0_), custom_call_target="tpu_custom_call" | custom-call | flops 1811939328 | bytes 12091392 | tf_op jit(solution)/shard_map/pallas_call | solution.py:257
  360.3 9.8 %shard_map.119.refs_1_ = bf16[192,768]{1,0:T(8,128)(2,1)S(1)} custom-call(s32[4]{0:T(128)S(1)} %get-tuple-element.45.order, bf16[768,6144]{1,0:T(8,128)(2,1)} %weight.19, bf16[1,4,192,1536]{3,2,1,0:T(8,128)(2,1)S(1)} %maximum_bitcast_fusion.refs_0_.refs_2_), custom_call_target="tpu_custom_call" | custom-call | flops 1811939328 | bytes 12091392 | tf_op jit(solution)/shard_map/pallas_call | solution.py:257
  370.2 8.9 %shard_map.122.refs_2_ = bf16[192,768]{1,0:T(8,128)(2,1)S(1)} custom-call(s32[4]{0:T(128)S(1)} %get-tuple-element.45.order, bf16[768,6144]{1,0:T(8,128)(2,1)} %weight.19, bf16[1,4,96,1536]{3,2,1,0:T(8,128)(2,1)S(1)} %copy-done.5, bf16[1,4,96,1536]{3,2,1,0:T(8,128)(2,1)S(1)} %copy-done.14), custom_call_target="tpu_custom_call" | custom-call | flops 1811939328 | bytes 12091392 | tf_op jit(solution)/shard_map/pallas_call | solution.py:257
  382.2 13.0 %shard_map.127 = bf16[768,6144]{1,0:T(8,128)(2,1)} custom-call(s32[4]{0:T(128)S(1)} %get-tuple-element.45.order, bf16[768,768]{1,0:T(8,128)(2,1)S(1)} %bitcast.107, bf16[1,4,96,1536]{3,2,1,0:T(8,128)(2,1)S(1)} %copy-done.4, bf16[1,4,96,1536]{3,2,1,0:T(8,128)(2,1)} %collective-permute-done.22.refs_1_.refs_0_, bf16[1,4,192,1536]{3,2,1,0:T(8,128)(2,1)} %copy-done.6, ...), custom_call_target="tpu_custom_call" | custom-call | flops 7247757312 | bytes 20054016 | tf_op jit(solution)/shard_map/pallas_call | solution.py:306
  397.7 8.9 %shard_map.126 = bf16[192,768]{1,0:T(8,128)(2,1)S(1)} custom-call(s32[4]{0:T(128)S(1)} %get-tuple-element.45.order, bf16[768,6144]{1,0:T(8,128)(2,1)} %weight.19, bf16[1,4,96,1536]{3,2,1,0:T(8,128)(2,1)S(1)} %copy-done.2, bf16[1,4,96,1536]{3,2,1,0:T(8,128)(2,1)S(1)} %copy-done.37), custom_call_target="tpu_custom_call" | custom-call | flops 1811939328 | bytes 12091392 | tf_op jit(solution)/shard_map/pallas_call | solution.py:257
  412.5 8.5 %collective-permute-done.32 = bf16[1,192,768]{2,1,0:T(8,128)(2,1)S(1)} collective-permute-done((bf16[1,192,768]{2,1,0:T(8,128)(2,1)S(1)}, bf16[1,192,768]{2,1,0:T(8,128)(2,1)S(1)}, u32[]{:S(2)}, u32[]{:S(2)}) %collective-permute-start.32) | collective-permute-done | bytes 294944 | tf_op jit(solution)/shard_map/ppermute | solution.py:39
  426.4 24.9 %collective-permute-done.33 = bf16[192,768]{1,0:T(8,128)(2,1)S(1)} collective-permute-done((bf16[192,768]{1,0:T(8,128)(2,1)S(1)}, bf16[192,768]{1,0:T(8,128)(2,1)S(1)}, u32[]{:S(2)}, u32[]{:S(2)}) %collective-permute-start.33) | collective-permute-done | bytes 294944 | tf_op jit(solution)/shard_map/ppermute | solution.py:508
  (282 shorter events, 143.0 us)
Async XLA Ops:
  7.2 40.3 %all-gather.2.cloned.1.call-start = ((), (), s32[]{:S(2)}) async-start(), calls=%async_computation.2 | async-start | bytes 1474560 | tf_op jit(solution)/shard_map/all_gather | solution.py:379
  29.3 377.5 %reduce-scatter.3.cloned.1.call-start = ((), (), s32[]{:S(2)}) async-start(), calls=%async_computation.3 | async-start | bytes 5898240 | tf_op jit(solution)/shard_map/reduce_scatter | solution.py:519
  59.9 40.7 %collective-permute-start.1 = (bf16[1,4,96,1536]{3,2,1,0:T(8,128)(2,1)S(1)}, bf16[1,4,96,1536]{3,2,1,0:T(8,128)(2,1)}, u32[]{:S(2)}, u32[]{:S(2)}) collective-permute-start(bf16[1,4,96,1536]{3,2,1,0:T(8,128)(2,1)S(1)} %get-tuple-element.13.refs_0_), channel_id=1, source_target_pairs={{0,1},{1,0},{2,3},{3,2},{4,5},{5,4},{6,7},{7,6},{8,9},{9,8},{10,11... | collective-permute-start | bytes 3538952 | tf_op jit(solution)/shard_map/ppermute | solution.py:39
  68.1 33.6 %collective-permute-start.4 = (bf16[2,192,1536]{2,1,0:T(8,128)(2,1)}, bf16[2,192,1536]{2,1,0:T(8,128)(2,1)}, u32[]{:S(2)}, u32[]{:S(2)}) collective-permute-start(bf16[2,192,1536]{2,1,0:T(8,128)(2,1)} %shard_map.97), channel_id=1, source_target_pairs={{0,8},{8,0},{16,24},{24,16},{1,9},{9,1},{17,25},{25,17},{2,10},{10... | collective-permute-start | bytes 3538952 | tf_op jit(solution)/shard_map/ppermute | solution.py:39
  72.4 35.9 %collective-permute-start.15 = (bf16[1,768,768]{2,1,0:T(8,128)(2,1)}, bf16[1,768,768]{2,1,0:T(8,128)(2,1)}, u32[]{:S(2)}, u32[]{:S(2)}) collective-permute-start(bf16[1,768,768]{2,1,0:T(8,128)(2,1)} %shard_map.109), channel_id=1, source_target_pairs={{0,4},{2,6},{4,0},{6,2},{1,5},{3,7},{5,1},{7,3},{8,12},{10,14},{12... | collective-permute-start | bytes 3538952 | tf_op jit(solution)/shard_map/ppermute | solution.py:39
  100.6 34.1 %collective-permute-start.6 = (bf16[1,4,96,1536]{3,2,1,0:T(8,128)(2,1)}, bf16[1,4,96,1536]{3,2,1,0:T(8,128)(2,1)S(1)}, u32[]{:S(2)}, u32[]{:S(2)}) collective-permute-start(bf16[1,4,96,1536]{3,2,1,0:T(8,128)(2,1)} %shard_map.102), channel_id=1, source_target_pairs={{0,1},{1,0},{2,3},{3,2},{4,5},{5,4},{6,7},{7,6},{8,9},{9,8},{10,11... | collective-permute-start | bytes 3538952 | tf_op jit(solution)/shard_map/ppermute | solution.py:39
  103.4 28.3 %collective-permute-start.5 = (bf16[1,192,1536]{2,1,0:T(8,128)(2,1)S(1)}, bf16[1,192,1536]{2,1,0:T(8,128)(2,1)S(1)}, u32[]{:S(2)}, u32[]{:S(2)}) collective-permute-start(bf16[1,192,1536]{2,1,0:T(8,128)(2,1)S(1)} %slice.188), channel_id=1, source_target_pairs={{0,16},{8,24},{16,0},{24,8},{1,17},{9,25},{17,1},{25,9},{2,18},{10... | collective-permute-start | bytes 1769480 | tf_op jit(solution)/shard_map/ppermute | solution.py:39
  107.6 27.0 %collective-permute-start.2 = (bf16[2,96,1536]{2,1,0:T(8,128)(2,1)S(1)}, bf16[2,96,1536]{2,1,0:T(8,128)(2,1)S(1)}, u32[]{:S(2)}, u32[]{:S(2)}) collective-permute-start(bf16[2,96,1536]{2,1,0:T(8,128)(2,1)S(1)} %slice.189), channel_id=1, source_target_pairs={{0,8},{8,0},{16,24},{24,16},{1,9},{9,1},{17,25},{25,17},{2,10},{10... | collective-permute-start | bytes 1769480 | tf_op jit(solution)/shard_map/ppermute | solution.py:39
  111.7 48.9 %collective-permute-start.16 = (bf16[2,768,768]{2,1,0:T(8,128)(2,1)}, bf16[2,768,768]{2,1,0:T(8,128)(2,1)}, u32[]{:S(2)}, u32[]{:S(2)}) collective-permute-start(bf16[2,768,768]{2,1,0:T(8,128)(2,1)} %pad_maximum_fusion.1), channel_id=1, source_target_pairs={{0,2},{2,0},{4,6},{6,4},{1,3},{3,1},{5,7},{7,5},{8,10},{10,8},{12,... | collective-permute-start | bytes 7077896 | tf_op jit(solution)/shard_map/ppermute | solution.py:39
  139.3 26.9 %collective-permute-start.7 = (bf16[1,4,96,1536]{3,2,1,0:T(8,128)(2,1)}, bf16[1,4,96,1536]{3,2,1,0:T(8,128)(2,1)}, u32[]{:S(2)}, u32[]{:S(2)}) collective-permute-start(bf16[1,4,96,1536]{3,2,1,0:T(8,128)(2,1)} %shard_map.103), channel_id=1, source_target_pairs={{0,1},{1,0},{2,3},{3,2},{4,5},{5,4},{6,7},{7,6},{8,9},{9,8},{10,11... | collective-permute-start | bytes 3538952 | tf_op jit(solution)/shard_map/ppermute | solution.py:39
  158.9 31.8 %collective-permute-start.10 = (bf16[1,96,1536]{2,1,0:T(8,128)(2,1)}, bf16[1,96,1536]{2,1,0:T(8,128)(2,1)}, u32[]{:S(2)}, u32[]{:S(2)}) collective-permute-start(bf16[1,96,1536]{2,1,0:T(8,128)(2,1)} %slice.192), channel_id=1, source_target_pairs={{0,16},{8,24},{16,0},{24,8},{1,17},{9,25},{17,1},{25,9},{2,18},{10... | collective-permute-start | bytes 884744 | tf_op jit(solution)/shard_map/ppermute | solution.py:39
  188.3 25.6 %collective-permute-start.17 = (bf16[1,384,1536]{2,1,0:T(8,128)(2,1)}, bf16[1,384,1536]{2,1,0:T(8,128)(2,1)S(1)}, u32[]{:S(2)}, u32[]{:S(2)}) collective-permute-start(bf16[1,384,1536]{2,1,0:T(8,128)(2,1)} %shard_map.111), channel_id=1, source_target_pairs={{0,1},{1,0},{2,3},{3,2},{4,5},{5,4},{6,7},{7,6},{8,9},{9,8},{10,11... | collective-permute-start | bytes 3538952 | tf_op jit(solution)/shard_map/ppermute | solution.py:39
  218.0 33.8 %collective-permute-start.18 = (bf16[1,384,1536]{2,1,0:T(8,128)(2,1)}, bf16[1,384,1536]{2,1,0:T(8,128)(2,1)S(1)}, u32[]{:S(2)}, u32[]{:S(2)}) collective-permute-start(bf16[1,384,1536]{2,1,0:T(8,128)(2,1)} %bitcast.114), channel_id=1, source_target_pairs={{0,1},{1,0},{2,3},{3,2},{4,5},{5,4},{6,7},{7,6},{8,9},{9,8},{10,11... | collective-permute-start | bytes 3538952 | tf_op jit(solution)/shard_map/ppermute | solution.py:39
  270.0 181.2 %reduce-scatter.5.cloned.1.call-start = ((), (), s32[]{:S(2)}) async-start(), calls=%async_computation.4 | async-start | bytes 1474560 | tf_op jit(solution)/shard_map/reduce_scatter | solution.py:523
  270.1 36.9 %collective-permute-start.22 = (bf16[1,4,96,1536]{3,2,1,0:T(8,128)(2,1)}, bf16[1,4,96,1536]{3,2,1,0:T(8,128)(2,1)}, u32[]{:S(2)}, u32[]{:S(2)}) collective-permute-start(bf16[1,4,96,1536]{3,2,1,0:T(8,128)(2,1)} %shard_map.116.refs_0_), channel_id=1, source_target_pairs={{0,1},{1,0},{2,3},{3,2},{4,5},{5,4},{6,7},{7,6},{8,9},{9,8},{10,11... | collective-permute-start | bytes 3538952 | tf_op jit(solution)/shard_map/ppermute | solution.py:39
  273.7 28.6 %collective-permute-start.23 = (bf16[1,96,1536]{2,1,0:T(8,128)(2,1)S(1)}, bf16[1,96,1536]{2,1,0:T(8,128)(2,1)S(1)}, u32[]{:S(2)}, u32[]{:S(2)}) collective-permute-start(bf16[1,96,1536]{2,1,0:T(8,128)(2,1)S(1)} %bitcast.105), channel_id=1, source_target_pairs={{0,1},{1,0},{2,3},{3,2},{4,5},{5,4},{6,7},{7,6},{8,9},{9,8},{10,11... | collective-permute-start | bytes 884744 | tf_op jit(solution)/shard_map/ppermute | solution.py:39
  275.5 30.1 %collective-permute-start.27 = (bf16[1,96,1536]{2,1,0:T(8,128)(2,1)S(1)}, bf16[1,96,1536]{2,1,0:T(8,128)(2,1)S(1)}, u32[]{:S(2)}, u32[]{:S(2)}) collective-permute-start(bf16[1,96,1536]{2,1,0:T(8,128)(2,1)S(1)} %bitcast.95), channel_id=1, source_target_pairs={{0,16},{8,24},{16,0},{24,8},{1,17},{9,25},{17,1},{25,9},{2,18},{10... | collective-permute-start | bytes 884744 | tf_op jit(solution)/shard_map/ppermute | solution.py:39
  278.5 27.3 %collective-permute-start.26 = (bf16[2,96,1536]{2,1,0:T(8,128)(2,1)S(1)}, bf16[2,96,1536]{2,1,0:T(8,128)(2,1)S(1)}, u32[]{:S(2)}, u32[]{:S(2)}) collective-permute-start(bf16[2,96,1536]{2,1,0:T(8,128)(2,1)S(1)} %copy-done.57), channel_id=1, source_target_pairs={{0,8},{8,0},{16,24},{24,16},{1,9},{9,1},{17,25},{25,17},{2,10},{10... | collective-permute-start | bytes 1769480 | tf_op jit(solution)/shard_map/ppermute | solution.py:39
  302.4 26.5 %collective-permute-start.24 = (bf16[1,192,1536]{2,1,0:T(8,128)(2,1)S(1)}, bf16[1,192,1536]{2,1,0:T(8,128)(2,1)S(1)}, u32[]{:S(2)}, u32[]{:S(2)}) collective-permute-start(bf16[1,192,1536]{2,1,0:T(8,128)(2,1)S(1)} %bitcast.116), channel_id=1, source_target_pairs={{0,16},{8,24},{16,0},{24,8},{1,17},{9,25},{17,1},{25,9},{2,18},{10... | collective-permute-start | bytes 1769480 | tf_op jit(solution)/shard_map/ppermute | solution.py:39
  305.7 24.5 %collective-permute-start.29 = (bf16[2,96,1536]{2,1,0:T(8,128)(2,1)S(1)}, bf16[2,96,1536]{2,1,0:T(8,128)(2,1)}, u32[]{:S(2)}, u32[]{:S(2)}) collective-permute-start(bf16[2,96,1536]{2,1,0:T(8,128)(2,1)S(1)} %pad_maximum_fusion.16.refs_1_), channel_id=1, source_target_pairs={{0,8},{8,0},{16,24},{24,16},{1,9},{9,1},{17,25},{25,17},{2,10},{10... | collective-permute-start | bytes 1769480 | tf_op jit(solution)/shard_map/ppermute | solution.py:39
  307.0 46.7 %collective-permute-start.28 = (bf16[1,4,96,1536]{3,2,1,0:T(8,128)(2,1)}, bf16[1,4,96,1536]{3,2,1,0:T(8,128)(2,1)S(1)}, u32[]{:S(2)}, u32[]{:S(2)}) collective-permute-start(bf16[1,4,96,1536]{3,2,1,0:T(8,128)(2,1)} %shard_map.121.refs_0_.refs_3_), channel_id=1, source_target_pairs={{0,1},{1,0},{2,3},{3,2},{4,5},{5,4},{6,7},{7,6},{8,9},{9,8},{10,11... | collective-permute-start | bytes 3538952 | tf_op jit(solution)/shard_map/ppermute | solution.py:39
  330.2 28.3 %collective-permute-start.25 = (bf16[2,192,1536]{2,1,0:T(8,128)(2,1)}, bf16[2,192,1536]{2,1,0:T(8,128)(2,1)}, u32[]{:S(2)}, u32[]{:S(2)}) collective-permute-start(bf16[2,192,1536]{2,1,0:T(8,128)(2,1)} %pad_maximum_fusion.9), channel_id=1, source_target_pairs={{0,8},{8,0},{16,24},{24,16},{1,9},{9,1},{17,25},{25,17},{2,10},{10... | collective-permute-start | bytes 3538952 | tf_op jit(solution)/shard_map/ppermute | solution.py:39
  354.7 26.5 %collective-permute-start.30 = (bf16[1,4,96,1536]{3,2,1,0:T(8,128)(2,1)}, bf16[1,4,96,1536]{3,2,1,0:T(8,128)(2,1)S(1)}, u32[]{:S(2)}, u32[]{:S(2)}) collective-permute-start(bf16[1,4,96,1536]{3,2,1,0:T(8,128)(2,1)} %shard_map.124.block.refs_5_), channel_id=1, source_target_pairs={{0,1},{1,0},{2,3},{3,2},{4,5},{5,4},{6,7},{7,6},{8,9},{9,8},{10,11... | collective-permute-start | bytes 3538952 | tf_op jit(solution)/shard_map/ppermute | solution.py:39
  421.1 30.2 %collective-permute-start.33 = (bf16[192,768]{1,0:T(8,128)(2,1)S(1)}, bf16[192,768]{1,0:T(8,128)(2,1)S(1)}, u32[]{:S(2)}, u32[]{:S(2)}) collective-permute-start(bf16[192,768]{1,0:T(8,128)(2,1)S(1)} %fusion.1), channel_id=1, source_target_pairs={{0,0},{2,8},{4,16},{6,24},{8,2},{10,10},{12,18},{14,26},{16,4},{18... | collective-permute-start | bytes 884744 | tf_op jit(solution)/shard_map/ppermute | solution.py:508
  (80 other events, 708.8 us)
Sparse Core Ops, SparseCore 0:
  29.4 18.0 all-gather.1
  270.1 46.9 reduce-scatter.2
  409.5 33.7 reduce-scatter.4

commit v2 on v1

--- a/solution.py
+++ b/solution.py
@@ -391,24 +391,32 @@
     across = [chunk for chunk in range(chunks) if crosswise[chunk]]
     rows_of = [shuffled[c * nk * count : (c + 1) * nk * count] for c in range(chunks)]
     kept = {}
-    for chunk in straight:
-        rows = rows_of[chunk]
-        if chunk != straight[0]:
+    arrived = []
+
+    def product(place):
+        rows = rows_of[straight[place]]
+        if place == 1:
             rows = after(rows, kept[straight[0]][1])
-        kept[chunk] = up_parts(order, rows, in_weight, nk // 2, count, ni)
-    totals = {}
+        if place > 1:
+            rows = after(rows, arrived[place - 2])
+        kept[straight[place]] = up_parts(order, rows, in_weight, nk // 2, count, ni)
+
+    product(0)
+    if len(straight) > 1:
+        product(1)
+    begun = kept[straight[:2][-1]][1]
+    crossing = {}
     for chunk in across:
-        rows = after(rows_of[chunk], kept[straight[0]][1])
+        rows = after(rows_of[chunk], begun)
         send = up_blocks(order[half:], rows, in_weight, ni, jnp.bfloat16)
         keep = up_blocks(order[:half], rows, in_weight, ni, jnp.float32)
-        keep, got = halved(keep, send, "ia", ni, 1, False)
-        totals[chunk] = (keep + got.astype(jnp.float32)).reshape(nk, count, -1)
+        crossing[chunk] = halved(keep, send, "ia", ni, 1, False)
 
     if ni == nj:
         cotangent = after(cotangent, turned)
     cot_tokens = relative(natural(doubled(cotangent[None], "ia", ni)), own_i)
     cot_tokens = relative(cot_tokens.reshape(nk, share, -1), own_k)
-    cot_tokens = after(cot_tokens.reshape(1, tokens, -1), kept[straight[0]][1])
+    cot_tokens = after(cot_tokens.reshape(1, tokens, -1), begun)
     cot_parts = doubled(cot_tokens, "ja", nj)
     cot_order = own_j ^ jnp.array(reversed_bits(nj), jnp.int32)
     if cot_parts.shape[-1] % 128:
@@ -418,61 +426,78 @@
     grad_keep, grad_send = down_parts(cot_order, cot_parts, out_weight, nk)
 
     sums = [None] * chunks
-    came = None
-    for chunk in straight + across:
-        if crosswise[chunk]:
-            total = totals[chunk]
-            send = after(total[nk // 2 :].astype(jnp.bfloat16), came)
-            sums[chunk] = halved(total[: nk // 2], send, "ka", nk, nk // 2, True)
-            came = sums[chunk][1]
-        else:
-            keep, send = kept[chunk]
-            send = send if came is None else after(send, came)
-            keep, came = halved(keep, send, "ka", nk, nk // 2, True)
-            total = keep + came.astype(jnp.float32)
-            sums[chunk] = halved(
-                total[:half], total[half:].astype(jnp.bfloat16), "ia", ni, 1, False
-            )
+    for place, chunk in enumerate(straight):
+        if place > 1:
+            product(place)
+        keep, send = kept[chunk]
+        if place:
+            send = after(send, arrived[-1])
+        keep, came = halved(keep, send, "ka", nk, nk // 2, True)
+        arrived.append(came)
+        total = keep + came.astype(jnp.float32)
+        sums[chunk] = halved(
+            total[:half], total[half:].astype(jnp.bfloat16), "ia", ni, 1, False
+        )
+    came = arrived[-1]
+    for chunk, later in zip(straight, arrived[1:]):
+        keep, got = sums[chunk]
+        sums[chunk] = keep, after(got, later)
+    for chunk in across:
+        keep, got = crossing[chunk]
+        got = after(got, arrived[-2:][0])
+        total = (keep + got.astype(jnp.float32)).reshape(nk, count, -1)
+        send = after(total[nk // 2 :].astype(jnp.bfloat16), came, grad_send)
+        sums[chunk] = halved(total[: nk // 2], send, "ka", nk, nk // 2, True)
+        came = sums[chunk][1]
     grad_keep, grad_got = halved(
         grad_keep, after(grad_send, came), "ka", nk, nk // 2, True
     )
     actives = [on_chunk(active_kernel, sums[chunk], 0) for chunk in range(chunks)]
     parts = after(jnp.concatenate(actives, axis=0), grad_got)[None]
-    active_rows = doubled(parts, "ka", nk, True).reshape(tokens, -1)
-    came = active_rows
-
-    firsts = {}
-    for chunk in straight + across:
+    active_parts = doubled(parts, "ka", nk, True)
+    active_rows = active_parts.reshape(tokens, -1)
+    came = active_parts
+
+    slopes = {}
+    slope = None
+    for chunk in range(chunks):
         arrays = list(sums[chunk]) + [grad_keep, grad_got]
-        block = on_chunk(slope_kernel, arrays, chunk)[None]
-        if crosswise[chunk]:
-            block = doubled(block, "ka", nk, True).reshape(1, nk * count, -1)
-        bit = ni // 2
-        firsts[chunk] = jnp.concatenate([block, flip(block, "ia", ni, bit)], axis=0)
-    turned_blocks = {}
-    for chunk in straight + across:
-        block = firsts[chunk]
-        bit = ni // 4
-        while bit:
-            block = jnp.concatenate([block, flip(block, "ia", ni, bit)], axis=0)
-            bit //= 2
-        turned_blocks[chunk] = block
-
-    columns = active_rows.T
-    out_weight_grad = weight_parts(
-        cot_order, columns, [cot_parts[None]], cot_parts.shape[0]
-    )
-    pieces_of = {}
-    input_rows = [None] * chunks
-    for place, chunk in enumerate(straight):
-        earlier = [came]
-        if place + 1 < len(straight):
-            earlier.append(firsts[straight[place + 1]])
-        if place == 0:
-            gate = earlier[-1]
-        if place == 2:
-            earlier += [input_rows[straight[0]], out_weight_grad]
-        block = after(turned_blocks[chunk][None], *earlier)
+        if slope is not None:
+            arrays[1] = after(arrays[1], slope)
+        slope = on_chunk(slope_kernel, arrays, chunk)
+        slopes[chunk] = slope[None]
+    gathered = [
+        lax.all_gather(slopes[chunk], "ia", axis=0, tiled=True) for chunk in range(chunks)
+    ]
+    plain = jnp.arange(ni, dtype=jnp.int32)
+
+    def output_over_ja(*gates):
+        active_tokens = relative(active_parts, own_k).reshape(ni, tokens // ni, -1)
+        active_tokens = natural(relative(active_tokens, own_i)).reshape(tokens, -1)
+        active_tokens = after(active_tokens, *gates)
+        if out_weight.shape[1] // nj % 128:
+            output_part = jnp.dot(
+                active_tokens, out_weight, preferred_element_type=jnp.float32
+            )
+            output_sum = lax.psum_scatter(
+                output_part.astype(jnp.bfloat16), "ja", scatter_dimension=1, tiled=True
+            ).astype(jnp.float32)
+        else:
+            send = up_blocks(
+                cot_order[nj // 2 :], active_tokens, out_weight, nj, jnp.bfloat16
+            )
+            keep = up_blocks(
+                cot_order[: nj // 2], active_tokens, out_weight, nj, jnp.float32
+            )
+            keep, got = halved(keep, send, "ja", nj, 1, False)
+            output_sum = keep + got.astype(jnp.float32)
+        return output_sum
+
+    pieces_of = []
+    input_rows = []
+    for chunk in range(chunks):
+        ready = slopes[chunks - 1] if chunk == 0 else came
+        block = after(gathered[chunk][None], came, ready, *input_rows[-2:-1])
         pieces = [block]
         bit = 1
         while bit < nk:
@@ -481,21 +506,23 @@
             bit *= 2
             if bit < nk:
                 block = jnp.concatenate([block, came], axis=0)
-        pieces_of[chunk] = pieces
-        if place == len(straight) - 1:
-            for other in across:
-                block = turned_blocks[other]
-                pieces_of[other] = [block.reshape(1, ni, nk * count, -1)]
-                input_rows[other] = input_parts(order, pieces_of[other], in_weight, ni)
-            done = [rows for rows in input_rows if rows is not None]
-            if done:
-                pieces = [after(pieces[0], *done)] + pieces[1:]
-        input_rows[chunk] = input_parts(order, pieces, in_weight, ni)
+        arrived.append(came)
+        pieces_of.append(pieces)
+        if chunk == 0:
+            output_sum = output_over_ja(came, gathered[: chunks // 2][-1])
+        if chunk == chunks - 1:
+            pieces = [after(pieces[0], output_sum, *input_rows)] + pieces[1:]
+        input_rows.append(input_parts(plain, pieces, in_weight, ni))
+    last_rows = input_rows[-1]
+    late = arrived[-2:][0]
+    out_weight_grad = weight_parts(
+        cot_order, after(active_rows.T, late), [cot_parts[None]], cot_parts.shape[0]
+    )
     input_rows = [rows.reshape(nk, count, depth) for rows in input_rows]
     in_weight_grad = weight_parts(
-        order,
-        shuffled.T,
-        [piece for chunk in range(chunks) for piece in pieces_of[chunk]],
+        plain,
+        after(shuffled.T, last_rows),
+        [piece for pieces in pieces_of for piece in pieces],
         ni,
     )
 
@@ -514,15 +541,10 @@
             input_full, "ja", scatter_dimension=1, tiled=True
         )
 
-    active_rows = after(active_rows, gate)
-    output_part = jnp.dot(active_rows, out_weight, preferred_element_type=jnp.float32)
-    output_cols = lax.psum_scatter(
-        output_part.astype(jnp.bfloat16), "ja", scatter_dimension=1, tiled=True
-    )
-    output_cols = relative(output_cols.reshape(nk, share, -1), own_k)
-    layer_out = lax.psum_scatter(
-        output_cols.reshape(tokens, -1), "ia", scatter_dimension=0, tiled=True
-    )
+    output_sum = output_sum.reshape(ni, tokens // ni, -1)
+    send = output_sum[half:].astype(jnp.bfloat16)
+    keep, got = halved(output_sum[:half], send, "ia", ni, 1, False)
+    layer_out = (keep + got.astype(jnp.float32)).astype(jnp.bfloat16)
     return (layer_out, feature_grad, in_weight_grad, out_weight_grad)
 
 

time: 461 us -> 491 us (1.065)
  waiting for transfers between devices: 191 us -> 164 us
  local copies, waits for them, and re-layouts: 40.2 us -> 66.1 us
  starting transfers between devices: 44.4 us -> 63.6 us
  Pallas kernels: 121 us -> 136 us
  matrix products: 12.3 us -> 0 us
  other arithmetic: 35.1 us -> 41.2 us
    unnamed x136 -> x171, local copies, waits for them, and re-layouts: 23 us -> 45 us
    ppermute x1, waiting for transfers between devices: 24.9 us -> 2.94 us  [local(): feature_grad = lax.ppermute(input_sum, ('ia', 'ja'), swap)]
    ppermute x32 -> x28, starting transfers between devices: 34.5 us -> 52.4 us  [flip(): return lax.ppermute(block, axis, [(d, d ^ bit) for d in range(size)])]
    pallas_call x2 -> x4, Pallas kernels: 10.1 us -> 24.9 us  [up_blocks(): pl.pallas_call(block_kernel, grid_spec=pltpu.PrefetchScalarGridSpec(num_s...]
    dot_general x1 -> x0, matrix products: 12.3 us -> none  [local(): jnp.dot(active_rows, out_weight, preferred_element_type=jnp.float32)]
    add x5 -> x7, other arithmetic: 4.35 us -> 12.2 us  [halved(): total = keep + got.astype(jnp.float32)]
    broadcast_in_dim x3 -> x0, other arithmetic: 5.72 us -> none  [local(): block = after(turned_blocks[chunk][None], *earlier)]
    ppermute x32 -> x28, waiting for transfers between devices: 149 us -> 146 us  [flip(): return lax.ppermute(block, axis, [(d, d ^ bit) for d in range(size)])]
  transfers between devices with their start and end apart: 37 -> 35, of which waited for: 18 -> 18; matrix products, arithmetic and copies ran while one was open for 10% -> 13% of each run, Pallas kernels for 26% -> 26%
where the time goes in v2:
time: 491 us; the launch traced here: 486 us
  waiting for transfers between devices  164 us (33%)
  Pallas kernels  136 us (28%)
  local copies, waits for them, and re-layouts  66.1 us (13%)
  starting transfers between devices  63.6 us (13%)
  other arithmetic  41.2 us (8%)
  between operations  14.9 us (3%)
    ppermute x28, waiting for transfers between devices, flip(): return lax.ppermute(block, axis, [(d, d ^ bit) for d in range(size)])  146 us
    ppermute x28, starting transfers between devices, flip(): return lax.ppermute(block, axis, [(d, d ^ bit) for d in range(size)])  52.4 us
    unnamed x171, local copies, waits for them, and re-layouts  45 us
    pallas_call x4, Pallas kernels, input_parts(): pl.pallas_call(input_kernel, grid_spec=pltpu.PrefetchScalarGridSpec(num_s...  35.5 us
    pallas_call x4, Pallas kernels, up_blocks(): pl.pallas_call(block_kernel, grid_spec=pltpu.PrefetchScalarGridSpec(num_s...  24.9 us
    pallas_call x2, Pallas kernels, weight_parts(): pl.pallas_call(weight_kernel, grid_spec=pltpu.PrefetchScalarGridSpec(num_...  24.6 us
    pallas_call x3, Pallas kernels, up_parts(): pl.pallas_call(up_kernel, grid_spec=pltpu.PrefetchScalarGridSpec(num_scal...  24.6 us
    pallas_call x1, Pallas kernels, down_parts(): pl.pallas_call(down_kernel, grid_spec=pltpu.PrefetchScalarGridSpec(num_sc...  17.1 us
  transfers between devices with their start and end apart: 35, of which 18 were waited for; matrix products, arithmetic and copies ran while one was open for 13% of the time, Pallas kernels for 26%

profile of v2, /device:TPU:4, one launch (start us, length us, event | category | flops | bytes accessed | tf_op | source)
XLA Modules:
  0.0 486.3 jit_solution(4919891837158723395)
XLA Ops:
  13.3 15.2 %collective-permute-done.refs_0_ = bf16[192,768]{1,0:T(8,128)(2,1)S(1)} collective-permute-done((bf16[192,768]{1,0:T(8,128)(2,1)}, bf16[192,768]{1,0:T(8,128)(2,1)S(1)}, u32[]{:S(2)}, u32[]{:S(2)}) %collective-permute-start) | collective-permute-done | bytes 294944 | tf_op jit(solution)/shard_map/ppermute | solution.py:378
  29.4 14.1 %collective-permute-done.8 = bf16[1,192,768]{2,1,0:T(8,128)(2,1)S(1)} collective-permute-done((bf16[1,192,768]{2,1,0:T(8,128)(2,1)}, bf16[1,192,768]{2,1,0:T(8,128)(2,1)S(1)}, u32[]{:S(2)}, u32[]{:S(2)}) %collective-permute-start.8) | collective-permute-done | bytes 294944 | tf_op jit(solution)/shard_map/ppermute | solution.py:39
  44.7 11.5 %collective-permute-done.9 = bf16[2,192,768]{2,1,0:T(8,128)(2,1)S(1)} collective-permute-done((bf16[2,192,768]{2,1,0:T(8,128)(2,1)S(1)}, bf16[2,192,768]{2,1,0:T(8,128)(2,1)S(1)}, u32[]{:S(2)}, u32[]{:S(2)}) %collective-permute-start.9) | collective-permute-done | bytes 589856 | tf_op jit(solution)/shard_map/ppermute | solution.py:39
  59.7 8.2 %shard_map.93 = (f32[1,4,96,1536]{3,2,1,0:T(8,128)S(1)}, bf16[1,4,96,1536]{3,2,1,0:T(8,128)(2,1)S(1)}) custom-call(s32[4]{0:T(128)S(1)} %get-tuple-element.52.order, bf16[192,768]{1,0:T(8,128)(2,1)S(1)} %bitcast.105, bf16[768,6144]{1,0:T(8,128)(2,1)} %weight.23), custom_call_target="tpu_custom_call" | custom-call | flops 1811939328 | bytes 12976128 | tf_op jit(solution)/shard_map/pallas_call | solution.py:88
  71.8 8.2 %shard_map.95 = (f32[1,4,96,1536]{3,2,1,0:T(8,128)S(1)}, bf16[1,4,96,1536]{3,2,1,0:T(8,128)(2,1)S(1)}) custom-call(s32[4]{0:T(128)S(1)} %get-tuple-element.52.order, bf16[192,768]{1,0:T(8,128)(2,1)S(1)} %copy-done.40, bf16[768,6144]{1,0:T(8,128)(2,1)} %weight.23), custom_call_target="tpu_custom_call" | custom-call | flops 1811939328 | bytes 12976128 | tf_op jit(solution)/shard_map/pallas_call | solution.py:88
  97.9 9.3 %collective-permute-done.10 = bf16[1,768,768]{2,1,0:T(8,128)(2,1)} collective-permute-done((bf16[1,768,768]{2,1,0:T(8,128)(2,1)}, bf16[1,768,768]{2,1,0:T(8,128)(2,1)}, u32[]{:S(2)}, u32[]{:S(2)}) %collective-permute-start.10) | collective-permute-done | bytes 1179680 | tf_op jit(solution)/shard_map/ppermute | solution.py:39
  126.5 8.2 %shard_map.104 = (f32[1,4,96,1536]{3,2,1,0:T(8,128)S(1)}, bf16[1,4,96,1536]{3,2,1,0:T(8,128)(2,1)S(1)}) custom-call(s32[4]{0:T(128)S(1)} %get-tuple-element.52.order, bf16[192,768]{1,0:T(8,128)(2,1)S(1)} %copy-done.39, bf16[768,6144]{1,0:T(8,128)(2,1)} %weight.23), custom_call_target="tpu_custom_call" | custom-call | flops 1811939328 | bytes 12976128 | tf_op jit(solution)/shard_map/pallas_call | solution.py:88
  139.6 7.2 %collective-permute-done.6 = bf16[1,192,1536]{2,1,0:T(8,128)(2,1)} collective-permute-done((bf16[1,192,1536]{2,1,0:T(8,128)(2,1)}, bf16[1,192,1536]{2,1,0:T(8,128)(2,1)}, u32[]{:S(2)}, u32[]{:S(2)}) %collective-permute-start.6) | collective-permute-done | bytes 589856 | tf_op jit(solution)/shard_map/ppermute | solution.py:39
  157.0 17.1 %shard_map.108 = (f32[1,384,1536]{2,1,0:T(8,128)S(1)}, bf16[1,384,1536]{2,1,0:T(8,128)(2,1)S(1)}) custom-call(s32[4]{0:T(128)S(1)} %get-tuple-element.53.order, bf16[4,768,768]{2,1,0:T(8,128)(2,1)} %get-tuple-element.21.rows, bf16[1536,3072]{1,0:T(8,128)(2,1)} %weight.19), custom_call_target="tpu_custom_call" | custom-call | flops 7247757312 | bytes 27131904 | tf_op jit(solution)/shard_map/pallas_call | solution.py:171
  177.7 6.3 %collective-permute-done.12 = bf16[1,96,1536]{2,1,0:T(8,128)(2,1)S(1)} collective-permute-done((bf16[1,96,1536]{2,1,0:T(8,128)(2,1)}, bf16[1,96,1536]{2,1,0:T(8,128)(2,1)S(1)}, u32[]{:S(2)}, u32[]{:S(2)}) %collective-permute-start.12) | collective-permute-done | bytes 294944 | tf_op jit(solution)/shard_map/ppermute | solution.py:39
  225.3 27.0 %collective-permute-done.14 = bf16[1,96,1536]{2,1,0:T(8,128)(2,1)} collective-permute-done((bf16[1,96,1536]{2,1,0:T(8,128)(2,1)S(1)}, bf16[1,96,1536]{2,1,0:T(8,128)(2,1)}, u32[]{:S(2)}, u32[]{:S(2)}) %collective-permute-start.14) | collective-permute-done | bytes 294944 | tf_op jit(solution)/shard_map/ppermute | solution.py:39
  282.4 14.6 %collective-permute-done.18 = bf16[1,384,1536]{2,1,0:T(8,128)(2,1)} collective-permute-done((bf16[1,384,1536]{2,1,0:T(8,128)(2,1)}, bf16[1,384,1536]{2,1,0:T(8,128)(2,1)}, u32[]{:S(2)}, u32[]{:S(2)}) %collective-permute-start.18) | collective-permute-done | bytes 1179680 | tf_op jit(solution)/shard_map/ppermute | solution.py:39
  306.0 15.1 %collective-permute-done.19.refs_0_.refs_1_ = bf16[1,4,96,1536]{3,2,1,0:T(8,128)(2,1)S(1)} collective-permute-done((bf16[1,4,96,1536]{3,2,1,0:T(8,128)(2,1)}, bf16[1,4,96,1536]{3,2,1,0:T(8,128)(2,1)S(1)}, u32[]{:S(2)}, u32[]{:S(2)}) %collective-permute-start.19) | collective-permute-done | bytes 1179680 | tf_op jit(solution)/shard_map/ppermute | solution.py:39
  323.7 7.3 %shard_map.126 = bf16[2,768,768]{2,1,0:T(8,128)(2,1)} custom-call(s32[2]{0:T(128)S(1)} %get-tuple-element.48.order, bf16[768,1536]{1,0:T(8,128)(2,1)S(1)} %copy-done, bf16[1536,3072]{1,0:T(8,128)(2,1)} %weight.19), custom_call_target="tpu_custom_call" | custom-call | flops 3623878656 | bytes 9437184 | tf_op jit(solution)/shard_map/pallas_call | solution.py:124
  332.6 8.9 %shard_map.127.refs_2_.refs_1_ = bf16[192,768]{1,0:T(8,128)(2,1)S(1)} custom-call(s32[4]{0:T(128)S(1)} %iota.11.order, bf16[768,6144]{1,0:T(8,128)(2,1)} %weight.23, bf16[1,4,96,1536]{3,2,1,0:T(8,128)(2,1)S(1)} %copy-done.29, bf16[1,4,96,1536]{3,2,1,0:T(8,128)(2,1)S(1)} %copy-done.7), custom_call_target="tpu_custom_call" | custom-call | flops 1811939328 | bytes 12091392 | tf_op jit(solution)/shard_map/pallas_call | solution.py:257
  342.2 17.4 %collective-permute-done.24.refs_1_.refs_0_.refs_3_ = bf16[1,4,96,1536]{3,2,1,0:T(8,128)(2,1)S(1)} collective-permute-done((bf16[1,4,96,1536]{3,2,1,0:T(8,128)(2,1)}, bf16[1,4,96,1536]{3,2,1,0:T(8,128)(2,1)S(1)}, u32[]{:S(2)}, u32[]{:S(2)}) %collective-permute-start.24) | collective-permute-done | bytes 1179680 | tf_op jit(solution)/shard_map/ppermute | solution.py:39
  362.3 7.6 %shard_map.125 = f32[2,768,768]{2,1,0:T(8,128)} custom-call(s32[2]{0:T(128)S(1)} %get-tuple-element.49.order, bf16[768,1536]{1,0:T(8,128)(2,1)S(1)} %copy-done.1, bf16[1536,3072]{1,0:T(8,128)(2,1)} %weight.19), custom_call_target="tpu_custom_call" | custom-call | flops 3623878656 | bytes 9437184 | tf_op jit(solution)/shard_map/pallas_call | solution.py:124
  377.6 8.9 %shard_map.129.refs_2_ = bf16[192,768]{1,0:T(8,128)(2,1)S(1)} custom-call(s32[4]{0:T(128)S(1)} %iota.12.order, bf16[768,6144]{1,0:T(8,128)(2,1)} %weight.23, bf16[1,4,96,1536]{3,2,1,0:T(8,128)(2,1)S(1)} %copy-done.11, bf16[1,4,96,1536]{3,2,1,0:T(8,128)(2,1)S(1)} %copy-done.10), custom_call_target="tpu_custom_call" | custom-call | flops 1811939328 | bytes 12091392 | tf_op jit(solution)/shard_map/pallas_call | solution.py:257
  399.5 8.9 %shard_map.131.refs_3_ = bf16[192,768]{1,0:T(8,128)(2,1)S(1)} custom-call(s32[4]{0:T(128)S(1)} %iota.13.order, bf16[768,6144]{1,0:T(8,128)(2,1)} %weight.23, bf16[1,4,96,1536]{3,2,1,0:T(8,128)(2,1)S(1)} %copy-done.31, bf16[1,4,96,1536]{3,2,1,0:T(8,128)(2,1)S(1)} %copy-done.5), custom_call_target="tpu_custom_call" | custom-call | flops 1811939328 | bytes 12091392 | tf_op jit(solution)/shard_map/pallas_call | solution.py:257
  412.3 7.7 %collective-permute-start.22 = (bf16[2,192,768]{2,1,0:T(8,128)(2,1)}, bf16[2,192,768]{2,1,0:T(8,128)(2,1)}, u32[]{:S(2)}, u32[]{:S(2)}) collective-permute-start(bf16[2,192,768]{2,1,0:T(8,128)(2,1)} %bitcast.36), channel_id=1, source_target_pairs={{0,8},{8,0},{16,24},{24,16},{1,9},{9,1},{17,25},{25,17},{2,10},{10... | collective-permute-start | bytes 1769480 | tf_op jit(solution)/shard_map/ppermute | solution.py:39
  421.3 8.9 %shard_map.134.refs_0_ = bf16[192,768]{1,0:T(8,128)(2,1)S(1)} custom-call(s32[4]{0:T(128)S(1)} %iota.14.order, bf16[768,6144]{1,0:T(8,128)(2,1)} %weight.23, bf16[1,4,96,1536]{3,2,1,0:T(8,128)(2,1)S(1)} %copy-done.15, bf16[1,4,96,1536]{3,2,1,0:T(8,128)(2,1)} %collective-permute-done.26.refs_1_.refs_7_), custom_call_target="tpu_custom_call" | custom-call | flops 1811939328 | bytes 12091392 | tf_op jit(solution)/shard_map/pallas_call | solution.py:257
  433.0 11.6 %shard_map.138 = bf16[1536,3072]{1,0:T(8,128)(2,1)} custom-call(s32[4]{0:T(128)S(1)} %get-tuple-element.53.order, bf16[1536,768]{1,0:T(8,128)(2,1)S(1)} %copy-done.16, bf16[1,4,768,768]{3,2,1,0:T(8,128)(2,1)} %get-tuple-element.20.refs_0_), custom_call_target="tpu_custom_call" | custom-call | flops 7247757312 | bytes 16515072 | tf_op jit(solution)/shard_map/pallas_call | solution.py:306
  455.9 6.5 %collective-permute-start.29 = (bf16[192,768]{1,0:T(8,128)(2,1)S(1)}, bf16[192,768]{1,0:T(8,128)(2,1)S(1)}, u32[]{:S(2)}, u32[]{:S(2)}) collective-permute-start(bf16[192,768]{1,0:T(8,128)(2,1)S(1)} %fusion.7), channel_id=1, source_target_pairs={{0,0},{2,8},{4,16},{6,24},{8,2},{10,10},{12,18},{14,26},{16,4},{18... | collective-permute-start | bytes 884744 | tf_op jit(solution)/shard_map/ppermute | solution.py:535
  462.4 13.0 %shard_map.136 = bf16[768,6144]{1,0:T(8,128)(2,1)} custom-call(s32[4]{0:T(128)S(1)} %iota.15.order, bf16[768,768]{1,0:T(8,128)(2,1)S(1)} %copy-done.35, bf16[1,4,96,1536]{3,2,1,0:T(8,128)(2,1)S(1)} %copy-done.30, bf16[1,4,96,1536]{3,2,1,0:T(8,128)(2,1)S(1)} %copy-done.8, bf16[1,4,96,1536]{3,2,1,0:T(8,128)(2,1)S(1)} %copy-done.12, ...), custom_call_target="tpu_custom_call" | custom-call | flops 7247757312 | bytes 20054016 | tf_op jit(solution)/shard_map/pallas_call | solution.py:306
  (332 shorter events, 202.9 us)
Async XLA Ops:
  7.2 49.6 %all-gather.10.cloned.1.call-start = ((), (), s32[]{:S(2)}) async-start(), calls=%async_computation | async-start | bytes 1474560 | tf_op jit(solution)/shard_map/all_gather | solution.py:379
  29.3 271.0 %all-gather.12.cloned.1.call-start = ((), (), s32[]{:S(2)}) async-start(), calls=%async_computation.1 | async-start | bytes 1474560 | tf_op jit(solution)/shard_map/all_gather | solution.py:470
  69.3 26.3 %collective-permute-start.1 = (bf16[1,4,96,1536]{3,2,1,0:T(8,128)(2,1)S(1)}, bf16[1,4,96,1536]{3,2,1,0:T(8,128)(2,1)}, u32[]{:S(2)}, u32[]{:S(2)}) collective-permute-start(bf16[1,4,96,1536]{3,2,1,0:T(8,128)(2,1)S(1)} %get-tuple-element.13.refs_0_), channel_id=1, source_target_pairs={{0,1},{1,0},{2,3},{3,2},{4,5},{5,4},{6,7},{7,6},{8,9},{9,8},{10,11... | collective-permute-start | bytes 3538952 | tf_op jit(solution)/shard_map/ppermute | solution.py:39
  82.8 24.4 %collective-permute-start.10 = (bf16[1,768,768]{2,1,0:T(8,128)(2,1)}, bf16[1,768,768]{2,1,0:T(8,128)(2,1)}, u32[]{:S(2)}, u32[]{:S(2)}) collective-permute-start(bf16[1,768,768]{2,1,0:T(8,128)(2,1)} %shard_map.107), channel_id=1, source_target_pairs={{0,4},{2,6},{4,0},{6,2},{1,5},{3,7},{5,1},{7,3},{8,12},{10,14},{12... | collective-permute-start | bytes 3538952 | tf_op jit(solution)/shard_map/ppermute | solution.py:39
  89.3 25.9 %collective-permute-start.5 = (bf16[2,192,1536]{2,1,0:T(8,128)(2,1)}, bf16[2,192,1536]{2,1,0:T(8,128)(2,1)}, u32[]{:S(2)}, u32[]{:S(2)}) collective-permute-start(bf16[2,192,1536]{2,1,0:T(8,128)(2,1)} %shard_map.101), channel_id=1, source_target_pairs={{0,8},{8,0},{16,24},{24,16},{1,9},{9,1},{17,25},{25,17},{2,10},{10... | collective-permute-start | bytes 3538952 | tf_op jit(solution)/shard_map/ppermute | solution.py:39
  96.9 40.3 %collective-permute-start.4 = (bf16[1,4,96,1536]{3,2,1,0:T(8,128)(2,1)S(1)}, bf16[1,4,96,1536]{3,2,1,0:T(8,128)(2,1)S(1)}, u32[]{:S(2)}, u32[]{:S(2)}) collective-permute-start(bf16[1,4,96,1536]{3,2,1,0:T(8,128)(2,1)S(1)} %copy-done.14), channel_id=1, source_target_pairs={{0,1},{1,0},{2,3},{3,2},{4,5},{5,4},{6,7},{7,6},{8,9},{9,8},{10,11... | collective-permute-start | bytes 3538952 | tf_op jit(solution)/shard_map/ppermute | solution.py:39
  110.4 41.1 %collective-permute-start.11 = (bf16[2,768,768]{2,1,0:T(8,128)(2,1)}, bf16[2,768,768]{2,1,0:T(8,128)(2,1)}, u32[]{:S(2)}, u32[]{:S(2)}) collective-permute-start(bf16[2,768,768]{2,1,0:T(8,128)(2,1)} %pad_maximum_fusion.2), channel_id=1, source_target_pairs={{0,2},{2,0},{4,6},{6,4},{1,3},{3,1},{5,7},{7,5},{8,10},{10,8},{12,... | collective-permute-start | bytes 7077896 | tf_op jit(solution)/shard_map/ppermute | solution.py:39
  117.8 28.9 %collective-permute-start.6 = (bf16[1,192,1536]{2,1,0:T(8,128)(2,1)}, bf16[1,192,1536]{2,1,0:T(8,128)(2,1)}, u32[]{:S(2)}, u32[]{:S(2)}) collective-permute-start(bf16[1,192,1536]{2,1,0:T(8,128)(2,1)} %slice.245), channel_id=1, source_target_pairs={{0,16},{8,24},{16,0},{24,8},{1,17},{9,25},{17,1},{25,9},{2,18},{10... | collective-permute-start | bytes 1769480 | tf_op jit(solution)/shard_map/ppermute | solution.py:39
  124.8 61.5 %collective-permute-start.2 = (bf16[2,96,1536]{2,1,0:T(8,128)(2,1)}, bf16[2,96,1536]{2,1,0:T(8,128)(2,1)}, u32[]{:S(2)}, u32[]{:S(2)}) collective-permute-start(bf16[2,96,1536]{2,1,0:T(8,128)(2,1)} %slice.246), channel_id=1, source_target_pairs={{0,8},{8,0},{16,24},{24,16},{1,9},{9,1},{17,25},{25,17},{2,10},{10... | collective-permute-start | bytes 1769480 | tf_op jit(solution)/shard_map/ppermute | solution.py:39
  138.3 36.8 %collective-permute-start.7 = (bf16[1,4,96,1536]{3,2,1,0:T(8,128)(2,1)}, bf16[1,4,96,1536]{3,2,1,0:T(8,128)(2,1)S(1)}, u32[]{:S(2)}, u32[]{:S(2)}) collective-permute-start(bf16[1,4,96,1536]{3,2,1,0:T(8,128)(2,1)} %shard_map.105), channel_id=1, source_target_pairs={{0,1},{1,0},{2,3},{3,2},{4,5},{5,4},{6,7},{7,6},{8,9},{9,8},{10,11... | collective-permute-start | bytes 3538952 | tf_op jit(solution)/shard_map/ppermute | solution.py:39
  184.7 25.9 %collective-permute-start.17 = (bf16[1,384,1536]{2,1,0:T(8,128)(2,1)}, bf16[1,384,1536]{2,1,0:T(8,128)(2,1)S(1)}, u32[]{:S(2)}, u32[]{:S(2)}) collective-permute-start(bf16[1,384,1536]{2,1,0:T(8,128)(2,1)} %shard_map.114), channel_id=1, source_target_pairs={{0,1},{1,0},{2,3},{3,2},{4,5},{5,4},{6,7},{7,6},{8,9},{9,8},{10,11... | collective-permute-start | bytes 3538952 | tf_op jit(solution)/shard_map/ppermute | solution.py:39
  193.3 26.5 %collective-permute-start.13 = (bf16[2,96,1536]{2,1,0:T(8,128)(2,1)}, bf16[2,96,1536]{2,1,0:T(8,128)(2,1)}, u32[]{:S(2)}, u32[]{:S(2)}) collective-permute-start(bf16[2,96,1536]{2,1,0:T(8,128)(2,1)} %slice.244), channel_id=1, source_target_pairs={{0,8},{8,0},{16,24},{24,16},{1,9},{9,1},{17,25},{25,17},{2,10},{10... | collective-permute-start | bytes 1769480 | tf_op jit(solution)/shard_map/ppermute | solution.py:39
  213.0 92.9 %all-gather.14.cloned.1.call-start = ((), (), s32[]{:S(2)}) async-start(), calls=%async_computation.2 | async-start | bytes 1474560 | tf_op jit(solution)/shard_map/all_gather | solution.py:470
  216.5 40.7 %collective-permute-start.15 = (bf16[2,96,1536]{2,1,0:T(8,128)(2,1)}, bf16[2,96,1536]{2,1,0:T(8,128)(2,1)}, u32[]{:S(2)}, u32[]{:S(2)}) collective-permute-start(bf16[2,96,1536]{2,1,0:T(8,128)(2,1)} %slice.243), channel_id=1, source_target_pairs={{0,8},{8,0},{16,24},{24,16},{1,9},{9,1},{17,25},{25,17},{2,10},{10... | collective-permute-start | bytes 1769480 | tf_op jit(solution)/shard_map/ppermute | solution.py:39
  221.1 31.2 %collective-permute-start.14 = (bf16[1,96,1536]{2,1,0:T(8,128)(2,1)S(1)}, bf16[1,96,1536]{2,1,0:T(8,128)(2,1)}, u32[]{:S(2)}, u32[]{:S(2)}) collective-permute-start(bf16[1,96,1536]{2,1,0:T(8,128)(2,1)S(1)} %slice.250), channel_id=1, source_target_pairs={{0,16},{8,24},{16,0},{24,8},{1,17},{9,25},{17,1},{25,9},{2,18},{10... | collective-permute-start | bytes 884744 | tf_op jit(solution)/shard_map/ppermute | solution.py:39
  265.9 76.3 %all-gather.16.cloned.1.call-start = ((), (), s32[]{:S(2)}) async-start(), calls=%async_computation.3 | async-start | bytes 1474560 | tf_op jit(solution)/shard_map/all_gather | solution.py:470
  278.9 108.3 %all-gather.18.cloned.1.call-start = ((), (), s32[]{:S(2)}) async-start(), calls=%async_computation.4 | async-start | bytes 1474560 | tf_op jit(solution)/shard_map/all_gather | solution.py:470
  330.9 39.0 %collective-permute-start.20 = (bf16[2,768,768]{2,1,0:T(8,128)(2,1)}, bf16[2,768,768]{2,1,0:T(8,128)(2,1)}, u32[]{:S(2)}, u32[]{:S(2)}) collective-permute-start(bf16[2,768,768]{2,1,0:T(8,128)(2,1)} %shard_map.126), channel_id=1, source_target_pairs={{0,2},{2,0},{4,6},{6,4},{1,3},{3,1},{5,7},{7,5},{8,10},{10,8},{12,... | collective-permute-start | bytes 7077896 | tf_op jit(solution)/shard_map/ppermute | solution.py:39
  331.0 28.6 %collective-permute-start.24 = (bf16[1,4,96,1536]{3,2,1,0:T(8,128)(2,1)}, bf16[1,4,96,1536]{3,2,1,0:T(8,128)(2,1)S(1)}, u32[]{:S(2)}, u32[]{:S(2)}) collective-permute-start(bf16[1,4,96,1536]{3,2,1,0:T(8,128)(2,1)} %shard_map.128.refs_0_.refs_2_), channel_id=1, source_target_pairs={{0,1},{1,0},{2,3},{3,2},{4,5},{5,4},{6,7},{7,6},{8,9},{9,8},{10,11... | collective-permute-start | bytes 3538952 | tf_op jit(solution)/shard_map/ppermute | solution.py:39
  360.6 27.8 %collective-permute-start.25 = (bf16[1,4,96,1536]{3,2,1,0:T(8,128)(2,1)}, bf16[1,4,96,1536]{3,2,1,0:T(8,128)(2,1)S(1)}, u32[]{:S(2)}, u32[]{:S(2)}) collective-permute-start(bf16[1,4,96,1536]{3,2,1,0:T(8,128)(2,1)} %shard_map.130.refs_0_.refs_4_), channel_id=1, source_target_pairs={{0,1},{1,0},{2,3},{3,2},{4,5},{5,4},{6,7},{7,6},{8,9},{9,8},{10,11... | collective-permute-start | bytes 3538952 | tf_op jit(solution)/shard_map/ppermute | solution.py:39
  374.7 33.7 %collective-permute-start.21 = (bf16[1,768,768]{2,1,0:T(8,128)(2,1)}, bf16[1,768,768]{2,1,0:T(8,128)(2,1)}, u32[]{:S(2)}, u32[]{:S(2)}) collective-permute-start(bf16[1,768,768]{2,1,0:T(8,128)(2,1)} %slice.241), channel_id=1, source_target_pairs={{0,4},{2,6},{4,0},{6,2},{1,5},{3,7},{5,1},{7,3},{8,12},{10,14},{12... | collective-permute-start | bytes 3538952 | tf_op jit(solution)/shard_map/ppermute | solution.py:39
  389.5 30.6 %collective-permute-start.26 = (bf16[1,4,96,1536]{3,2,1,0:T(8,128)(2,1)}, bf16[1,4,96,1536]{3,2,1,0:T(8,128)(2,1)}, u32[]{:S(2)}, u32[]{:S(2)}) collective-permute-start(bf16[1,4,96,1536]{3,2,1,0:T(8,128)(2,1)} %shard_map.132.refs_6_), channel_id=1, source_target_pairs={{0,1},{1,0},{2,3},{3,2},{4,5},{5,4},{6,7},{7,6},{8,9},{9,8},{10,11... | collective-permute-start | bytes 3538952 | tf_op jit(solution)/shard_map/ppermute | solution.py:39
  412.3 36.6 %collective-permute-start.22 = (bf16[2,192,768]{2,1,0:T(8,128)(2,1)}, bf16[2,192,768]{2,1,0:T(8,128)(2,1)}, u32[]{:S(2)}, u32[]{:S(2)}) collective-permute-start(bf16[2,192,768]{2,1,0:T(8,128)(2,1)} %bitcast.36), channel_id=1, source_target_pairs={{0,8},{8,0},{16,24},{24,16},{1,9},{9,1},{17,25},{25,17},{2,10},{10... | collective-permute-start | bytes 1769480 | tf_op jit(solution)/shard_map/ppermute | solution.py:39
  450.3 25.0 %collective-permute-start.23 = (bf16[1,192,768]{2,1,0:T(8,128)(2,1)S(1)}, bf16[1,192,768]{2,1,0:T(8,128)(2,1)S(1)}, u32[]{:S(2)}, u32[]{:S(2)}) collective-permute-start(bf16[1,192,768]{2,1,0:T(8,128)(2,1)S(1)} %slice.248), channel_id=1, source_target_pairs={{0,16},{8,24},{16,0},{24,8},{1,17},{9,25},{17,1},{25,9},{2,18},{10... | collective-permute-start | bytes 884744 | tf_op jit(solution)/shard_map/ppermute | solution.py:39
  (95 other events, 514.8 us)
Sparse Core Ops, SparseCore 0:
  29.4 18.0 all-gather.9
  213.1 43.6 all-gather.11
  266.0 31.0 all-gather.13
  299.0 29.5 all-gather.15
  332.6 38.1 all-gather.17

commit v3 on v2

--- a/solution.py
+++ b/solution.py
@@ -453,17 +453,17 @@
         grad_keep, after(grad_send, came), "ka", nk, nk // 2, True
     )
     actives = [on_chunk(active_kernel, sums[chunk], 0) for chunk in range(chunks)]
-    parts = after(jnp.concatenate(actives, axis=0), grad_got)[None]
+    own_active = jnp.concatenate(actives, axis=0)
+    parts = after(own_active, grad_got)[None]
     active_parts = doubled(parts, "ka", nk, True)
     active_rows = active_parts.reshape(tokens, -1)
     came = active_parts
 
     slopes = {}
-    slope = None
+    slope = own_active
     for chunk in range(chunks):
         arrays = list(sums[chunk]) + [grad_keep, grad_got]
-        if slope is not None:
-            arrays[1] = after(arrays[1], slope)
+        arrays[1] = after(arrays[1], slope)
         slope = on_chunk(slope_kernel, arrays, chunk)
         slopes[chunk] = slope[None]
     gathered = [
@@ -511,13 +511,16 @@
         if chunk == 0:
             output_sum = output_over_ja(came, gathered[: chunks // 2][-1])
         if chunk == chunks - 1:
-            pieces = [after(pieces[0], output_sum, *input_rows)] + pieces[1:]
+            out_weight_grad = weight_parts(
+                cot_order,
+                after(active_rows.T, arrived[-2]),
+                [cot_parts[None]],
+                cot_parts.shape[0],
+            )
+            earlier = [output_sum, out_weight_grad] + input_rows
+            pieces = [after(pieces[0], *earlier)] + pieces[1:]
         input_rows.append(input_parts(plain, pieces, in_weight, ni))
     last_rows = input_rows[-1]
-    late = arrived[-2:][0]
-    out_weight_grad = weight_parts(
-        cot_order, after(active_rows.T, late), [cot_parts[None]], cot_parts.shape[0]
-    )
     input_rows = [rows.reshape(nk, count, depth) for rows in input_rows]
     in_weight_grad = weight_parts(
         plain,

time: 491 us -> 483 us (0.984)
  starting transfers between devices: 63.6 us -> 34.7 us
  waiting for transfers between devices: 164 us -> 181 us
  local copies, waits for them, and re-layouts: 66.1 us -> 72.7 us
    all_gather x4, waiting for transfers between devices: 0.01 us -> 36.2 us  [local(): lax.all_gather(slopes[chunk], 'ia', axis=0, tiled=True)]
    ppermute x28, waiting for transfers between devices: 146 us -> 120 us  [flip(): return lax.ppermute(block, axis, [(d, d ^ bit) for d in range(size)])]
    ppermute x28, starting transfers between devices: 52.4 us -> 26.4 us  [flip(): return lax.ppermute(block, axis, [(d, d ^ bit) for d in range(size)])]
    ppermute x1, waiting for transfers between devices: 2.94 us -> 9.8 us  [local(): feature_grad = lax.ppermute(input_sum, ('ia', 'ja'), swap)]
    unnamed x171 -> x173, local copies, waits for them, and re-layouts: 45 us -> 50.9 us
    pallas_call x8, Pallas kernels: 9.22 us -> 4.08 us  [on_chunk(): pl.pallas_call(kernel, grid=(span // tile,), in_specs=[here, here] + [the...]
  transfers between devices with their start and end apart: 35 -> 35, of which waited for: 18 -> 17; matrix products, arithmetic and copies ran while one was open for 13% -> 13% of each run, Pallas kernels for 26% -> 24%
where the time goes in v3:
time: 483 us; the launch traced here: 479 us
  waiting for transfers between devices  181 us (37%)
  Pallas kernels  132 us (27%)
  local copies, waits for them, and re-layouts  72.7 us (15%)
  other arithmetic  43.9 us (9%)
  starting transfers between devices  34.7 us (7%)
  between operations  14.8 us (3%)
    ppermute x28, waiting for transfers between devices, flip(): return lax.ppermute(block, axis, [(d, d ^ bit) for d in range(size)])  120 us
    unnamed x173, local copies, waits for them, and re-layouts  50.9 us
    all_gather x4, waiting for transfers between devices, local(): lax.all_gather(slopes[chunk], 'ia', axis=0, tiled=True)  36.2 us
    pallas_call x4, Pallas kernels, input_parts(): pl.pallas_call(input_kernel, grid_spec=pltpu.PrefetchScalarGridSpec(num_s...  35.8 us
    ppermute x28, starting transfers between devices, flip(): return lax.ppermute(block, axis, [(d, d ^ bit) for d in range(size)])  26.4 us
    pallas_call x3, Pallas kernels, up_parts(): pl.pallas_call(up_kernel, grid_spec=pltpu.PrefetchScalarGridSpec(num_scal...  25.6 us
    pallas_call x4, Pallas kernels, up_blocks(): pl.pallas_call(block_kernel, grid_spec=pltpu.PrefetchScalarGridSpec(num_s...  25.1 us
    pallas_call x2, Pallas kernels, weight_parts(): pl.pallas_call(weight_kernel, grid_spec=pltpu.PrefetchScalarGridSpec(num_...  24.5 us
  transfers between devices with their start and end apart: 35, of which 17 were waited for; matrix products, arithmetic and copies ran while one was open for 13% of the time, Pallas kernels for 24%

profile of v3, /device:TPU:4, one launch (start us, length us, event | category | flops | bytes accessed | tf_op | source)
XLA Modules:
  0.0 479.5 jit_solution(11149785102769360253)
XLA Ops:
  13.3 15.2 %collective-permute-done.refs_0_ = bf16[192,768]{1,0:T(8,128)(2,1)S(1)} collective-permute-done((bf16[192,768]{1,0:T(8,128)(2,1)}, bf16[192,768]{1,0:T(8,128)(2,1)S(1)}, u32[]{:S(2)}, u32[]{:S(2)}) %collective-permute-start) | collective-permute-done | bytes 294944 | tf_op jit(solution)/shard_map/ppermute | solution.py:378
  29.4 14.1 %collective-permute-done.8 = bf16[1,192,768]{2,1,0:T(8,128)(2,1)S(1)} collective-permute-done((bf16[1,192,768]{2,1,0:T(8,128)(2,1)}, bf16[1,192,768]{2,1,0:T(8,128)(2,1)S(1)}, u32[]{:S(2)}, u32[]{:S(2)}) %collective-permute-start.8) | collective-permute-done | bytes 294944 | tf_op jit(solution)/shard_map/ppermute | solution.py:39
  44.7 11.5 %collective-permute-done.9 = bf16[2,192,768]{2,1,0:T(8,128)(2,1)S(1)} collective-permute-done((bf16[2,192,768]{2,1,0:T(8,128)(2,1)S(1)}, bf16[2,192,768]{2,1,0:T(8,128)(2,1)S(1)}, u32[]{:S(2)}, u32[]{:S(2)}) %collective-permute-start.9) | collective-permute-done | bytes 589856 | tf_op jit(solution)/shard_map/ppermute | solution.py:39
  59.6 9.1 %shard_map.93 = (f32[1,4,96,1536]{3,2,1,0:T(8,128)S(1)}, bf16[1,4,96,1536]{3,2,1,0:T(8,128)(2,1)}) custom-call(s32[4]{0:T(128)S(1)} %get-tuple-element.52.order, bf16[192,768]{1,0:T(8,128)(2,1)S(1)} %bitcast.109, bf16[768,6144]{1,0:T(8,128)(2,1)} %weight.23), custom_call_target="tpu_custom_call" | custom-call | flops 1811939328 | bytes 12976128 | tf_op jit(solution)/shard_map/pallas_call | solution.py:88
  72.6 8.2 %shard_map.95 = (f32[1,4,96,1536]{3,2,1,0:T(8,128)S(1)}, bf16[1,4,96,1536]{3,2,1,0:T(8,128)(2,1)S(1)}) custom-call(s32[4]{0:T(128)S(1)} %get-tuple-element.52.order, bf16[192,768]{1,0:T(8,128)(2,1)S(1)} %copy-done.45, bf16[768,6144]{1,0:T(8,128)(2,1)} %weight.23), custom_call_target="tpu_custom_call" | custom-call | flops 1811939328 | bytes 12976128 | tf_op jit(solution)/shard_map/pallas_call | solution.py:88
  103.1 15.9 %collective-permute-done.5 = bf16[2,192,1536]{2,1,0:T(8,128)(2,1)} collective-permute-done((bf16[2,192,1536]{2,1,0:T(8,128)(2,1)}, bf16[2,192,1536]{2,1,0:T(8,128)(2,1)}, u32[]{:S(2)}, u32[]{:S(2)}) %collective-permute-start.5) | collective-permute-done | bytes 1179680 | tf_op jit(solution)/shard_map/ppermute | solution.py:39
  130.4 8.3 %shard_map.104 = (f32[1,4,96,1536]{3,2,1,0:T(8,128)S(1)}, bf16[1,4,96,1536]{3,2,1,0:T(8,128)(2,1)S(1)}) custom-call(s32[4]{0:T(128)S(1)} %get-tuple-element.52.order, bf16[192,768]{1,0:T(8,128)(2,1)S(1)} %copy-done.44, bf16[768,6144]{1,0:T(8,128)(2,1)} %weight.23), custom_call_target="tpu_custom_call" | custom-call | flops 1811939328 | bytes 12976128 | tf_op jit(solution)/shard_map/pallas_call | solution.py:88
  141.7 20.6 %collective-permute-done.3 = bf16[1,96,1536]{2,1,0:T(8,128)(2,1)S(1)} collective-permute-done((bf16[1,96,1536]{2,1,0:T(8,128)(2,1)S(1)}, bf16[1,96,1536]{2,1,0:T(8,128)(2,1)S(1)}, u32[]{:S(2)}, u32[]{:S(2)}) %collective-permute-start.3) | collective-permute-done | bytes 294944 | tf_op jit(solution)/shard_map/ppermute | solution.py:39
  194.7 17.1 %shard_map.108 = (f32[1,384,1536]{2,1,0:T(8,128)S(1)}, bf16[1,384,1536]{2,1,0:T(8,128)(2,1)S(1)}) custom-call(s32[4]{0:T(128)S(1)} %get-tuple-element.53.order, bf16[4,768,768]{2,1,0:T(8,128)(2,1)} %get-tuple-element.21.rows, bf16[1536,3072]{1,0:T(8,128)(2,1)} %weight.19), custom_call_target="tpu_custom_call" | custom-call | flops 7247757312 | bytes 27131904 | tf_op jit(solution)/shard_map/pallas_call | solution.py:171
  227.1 10.0 %collective-permute-done.16 = bf16[1,96,1536]{2,1,0:T(8,128)(2,1)S(1)} collective-permute-done((bf16[1,96,1536]{2,1,0:T(8,128)(2,1)S(1)}, bf16[1,96,1536]{2,1,0:T(8,128)(2,1)S(1)}, u32[]{:S(2)}, u32[]{:S(2)}) %collective-permute-start.16) | collective-permute-done | bytes 294944 | tf_op jit(solution)/shard_map/ppermute | solution.py:39
  260.7 13.8 %collective-permute-done.18 = bf16[1,384,1536]{2,1,0:T(8,128)(2,1)} collective-permute-done((bf16[1,384,1536]{2,1,0:T(8,128)(2,1)}, bf16[1,384,1536]{2,1,0:T(8,128)(2,1)}, u32[]{:S(2)}, u32[]{:S(2)}) %collective-permute-start.18) | collective-permute-done | bytes 1179680 | tf_op jit(solution)/shard_map/ppermute | solution.py:39
  283.8 25.5 %all-gather.14.cloned.1.call-done = bf16[384,1536]{1,0:T(8,128)(2,1)} async-done(((bf16[96,1536]{1,0:T(8,128)(2,1)}), bf16[384,1536]{1,0:T(8,128)(2,1)}) %all-gather.14.cloned.1.call-update) | async-done | bytes 1179664 | tf_op jit(solution)/shard_map/all_gather | solution.py:470
  312.0 7.2 %shard_map.127 = bf16[2,768,768]{2,1,0:T(8,128)(2,1)} custom-call(s32[2]{0:T(128)S(1)} %get-tuple-element.48.order, bf16[768,1536]{1,0:T(8,128)(2,1)S(1)} %copy-done, bf16[1536,3072]{1,0:T(8,128)(2,1)} %weight.19), custom_call_target="tpu_custom_call" | custom-call | flops 3623878656 | bytes 9437184 | tf_op jit(solution)/shard_map/pallas_call | solution.py:124
  320.9 8.9 %shard_map.128.refs_2_ = bf16[192,768]{1,0:T(8,128)(2,1)S(1)} custom-call(s32[4]{0:T(128)S(1)} %iota.11.order, bf16[768,6144]{1,0:T(8,128)(2,1)} %weight.23, bf16[1,4,96,1536]{3,2,1,0:T(8,128)(2,1)S(1)} %copy-done.27, bf16[1,4,96,1536]{3,2,1,0:T(8,128)(2,1)S(1)} %copy-done.7), custom_call_target="tpu_custom_call" | custom-call | flops 1811939328 | bytes 12091392 | tf_op jit(solution)/shard_map/pallas_call | solution.py:257
  330.5 10.4 %all-gather.16.cloned.1.call-done = bf16[384,1536]{1,0:T(8,128)(2,1)} async-done(((bf16[96,1536]{1,0:T(8,128)(2,1)}), bf16[384,1536]{1,0:T(8,128)(2,1)}) %all-gather.16.cloned.1.call-update) | async-done | bytes 1179664 | tf_op jit(solution)/shard_map/all_gather | solution.py:470
  340.9 6.9 %collective-permute-done.24.refs_1_.refs_0_.refs_3_ = bf16[1,4,96,1536]{3,2,1,0:T(8,128)(2,1)S(1)} collective-permute-done((bf16[1,4,96,1536]{3,2,1,0:T(8,128)(2,1)}, bf16[1,4,96,1536]{3,2,1,0:T(8,128)(2,1)S(1)}, u32[]{:S(2)}, u32[]{:S(2)}) %collective-permute-start.24) | collective-permute-done | bytes 1179680 | tf_op jit(solution)/shard_map/ppermute | solution.py:39
  350.6 7.6 %shard_map.126 = f32[2,768,768]{2,1,0:T(8,128)} custom-call(s32[2]{0:T(128)S(1)} %get-tuple-element.49.order, bf16[768,1536]{1,0:T(8,128)(2,1)S(1)} %copy-done.1, bf16[1536,3072]{1,0:T(8,128)(2,1)} %weight.19), custom_call_target="tpu_custom_call" | custom-call | flops 3623878656 | bytes 9437184 | tf_op jit(solution)/shard_map/pallas_call | solution.py:124
  372.5 8.9 %shard_map.130.refs_2_.refs_3_ = bf16[192,768]{1,0:T(8,128)(2,1)S(1)} custom-call(s32[4]{0:T(128)S(1)} %iota.12.order, bf16[768,6144]{1,0:T(8,128)(2,1)} %weight.23, bf16[1,4,96,1536]{3,2,1,0:T(8,128)(2,1)S(1)} %copy-done.12, bf16[1,4,96,1536]{3,2,1,0:T(8,128)(2,1)S(1)} %copy-done.11), custom_call_target="tpu_custom_call" | custom-call | flops 1811939328 | bytes 12091392 | tf_op jit(solution)/shard_map/pallas_call | solution.py:257
  387.9 9.1 %shard_map.132.refs_4_ = bf16[192,768]{1,0:T(8,128)(2,1)S(1)} custom-call(s32[4]{0:T(128)S(1)} %iota.13.order, bf16[768,6144]{1,0:T(8,128)(2,1)} %weight.23, bf16[1,4,96,1536]{3,2,1,0:T(8,128)(2,1)S(1)} %copy-done.26, bf16[1,4,96,1536]{3,2,1,0:T(8,128)(2,1)S(1)} %copy-done.5), custom_call_target="tpu_custom_call" | custom-call | flops 1811939328 | bytes 12091392 | tf_op jit(solution)/shard_map/pallas_call | solution.py:257
  397.0 11.5 %shard_map.135.refs_1_ = bf16[1536,3072]{1,0:T(8,128)(2,1)} custom-call(s32[4]{0:T(128)S(1)} %get-tuple-element.53.order, bf16[1536,768]{1,0:T(8,128)(2,1)S(1)} %copy-done.15, bf16[1,4,768,768]{3,2,1,0:T(8,128)(2,1)} %get-tuple-element.20.refs_0_), custom_call_target="tpu_custom_call" | custom-call | flops 7247757312 | bytes 16515072 | tf_op jit(solution)/shard_map/pallas_call | solution.py:306
  414.5 8.9 %shard_map.137.refs_0_ = bf16[192,768]{1,0:T(8,128)(2,1)S(1)} custom-call(s32[4]{0:T(128)S(1)} %iota.14.order, bf16[768,6144]{1,0:T(8,128)(2,1)} %weight.23, bf16[1,4,96,1536]{3,2,1,0:T(8,128)(2,1)S(1)} %copy-done.9, bf16[1,4,96,1536]{3,2,1,0:T(8,128)(2,1)} %collective-permute-done.26.refs_1_.refs_7_), custom_call_target="tpu_custom_call" | custom-call | flops 1811939328 | bytes 12091392 | tf_op jit(solution)/shard_map/pallas_call | solution.py:257
  432.0 10.6 %collective-permute-done.22 = bf16[2,192,768]{2,1,0:T(8,128)(2,1)} collective-permute-done((bf16[2,192,768]{2,1,0:T(8,128)(2,1)S(1)}, bf16[2,192,768]{2,1,0:T(8,128)(2,1)}, u32[]{:S(2)}, u32[]{:S(2)}) %collective-permute-start.22) | collective-permute-done | bytes 589856 | tf_op jit(solution)/shard_map/ppermute | solution.py:39
  448.7 13.0 %shard_map.139 = bf16[768,6144]{1,0:T(8,128)(2,1)} custom-call(s32[4]{0:T(128)S(1)} %iota.15.order, bf16[768,768]{1,0:T(8,128)(2,1)S(1)} %copy-done.38, bf16[1,4,96,1536]{3,2,1,0:T(8,128)(2,1)S(1)} %copy-done.28, bf16[1,4,96,1536]{3,2,1,0:T(8,128)(2,1)S(1)} %copy-done.8, bf16[1,4,96,1536]{3,2,1,0:T(8,128)(2,1)S(1)} %copy-done.13, ...), custom_call_target="tpu_custom_call" | custom-call | flops 7247757312 | bytes 20054016 | tf_op jit(solution)/shard_map/pallas_call | solution.py:306
  462.4 9.8 %collective-permute-done.29 = bf16[192,768]{1,0:T(8,128)(2,1)S(1)} collective-permute-done((bf16[192,768]{1,0:T(8,128)(2,1)S(1)}, bf16[192,768]{1,0:T(8,128)(2,1)S(1)}, u32[]{:S(2)}, u32[]{:S(2)}) %collective-permute-start.29) | collective-permute-done | bytes 294944 | tf_op jit(solution)/shard_map/ppermute | solution.py:538
  (336 shorter events, 182.4 us)
Async XLA Ops:
  7.2 49.6 %all-gather.10.cloned.1.call-start = ((), (), s32[]{:S(2)}) async-start(), calls=%async_computation | async-start | bytes 1474560 | tf_op jit(solution)/shard_map/all_gather | solution.py:379
  29.3 248.9 %all-gather.12.cloned.1.call-start = ((), (), s32[]{:S(2)}) async-start(), calls=%async_computation.1 | async-start | bytes 1474560 | tf_op jit(solution)/shard_map/all_gather | solution.py:470
  70.1 28.2 %collective-permute-start.1 = (bf16[1,4,96,1536]{3,2,1,0:T(8,128)(2,1)}, bf16[1,4,96,1536]{3,2,1,0:T(8,128)(2,1)}, u32[]{:S(2)}, u32[]{:S(2)}) collective-permute-start(bf16[1,4,96,1536]{3,2,1,0:T(8,128)(2,1)} %get-tuple-element.13.refs_0_), channel_id=1, source_target_pairs={{0,1},{1,0},{2,3},{3,2},{4,5},{5,4},{6,7},{7,6},{8,9},{9,8},{10,11... | collective-permute-start | bytes 3538952 | tf_op jit(solution)/shard_map/ppermute | solution.py:39
  89.7 29.2 %collective-permute-start.5 = (bf16[2,192,1536]{2,1,0:T(8,128)(2,1)}, bf16[2,192,1536]{2,1,0:T(8,128)(2,1)}, u32[]{:S(2)}, u32[]{:S(2)}) collective-permute-start(bf16[2,192,1536]{2,1,0:T(8,128)(2,1)} %shard_map.101), channel_id=1, source_target_pairs={{0,8},{8,0},{16,24},{24,16},{1,9},{9,1},{17,25},{25,17},{2,10},{10... | collective-permute-start | bytes 3538952 | tf_op jit(solution)/shard_map/ppermute | solution.py:39
  92.6 34.9 %collective-permute-start.10 = (bf16[1,768,768]{2,1,0:T(8,128)(2,1)}, bf16[1,768,768]{2,1,0:T(8,128)(2,1)}, u32[]{:S(2)}, u32[]{:S(2)}) collective-permute-start(bf16[1,768,768]{2,1,0:T(8,128)(2,1)} %shard_map.107), channel_id=1, source_target_pairs={{0,4},{2,6},{4,0},{6,2},{1,5},{3,7},{5,1},{7,3},{8,12},{10,14},{12... | collective-permute-start | bytes 3538952 | tf_op jit(solution)/shard_map/ppermute | solution.py:39
  102.2 37.6 %collective-permute-start.2 = (bf16[2,96,1536]{2,1,0:T(8,128)(2,1)}, bf16[2,96,1536]{2,1,0:T(8,128)(2,1)}, u32[]{:S(2)}, u32[]{:S(2)}) collective-permute-start(bf16[2,96,1536]{2,1,0:T(8,128)(2,1)} %slice.246), channel_id=1, source_target_pairs={{0,8},{8,0},{16,24},{24,16},{1,9},{9,1},{17,25},{25,17},{2,10},{10... | collective-permute-start | bytes 1769480 | tf_op jit(solution)/shard_map/ppermute | solution.py:39
  102.5 59.7 %collective-permute-start.4 = (bf16[1,4,96,1536]{3,2,1,0:T(8,128)(2,1)}, bf16[1,4,96,1536]{3,2,1,0:T(8,128)(2,1)}, u32[]{:S(2)}, u32[]{:S(2)}) collective-permute-start(bf16[1,4,96,1536]{3,2,1,0:T(8,128)(2,1)} %shard_map.96), channel_id=1, source_target_pairs={{0,1},{1,0},{2,3},{3,2},{4,5},{5,4},{6,7},{7,6},{8,9},{9,8},{10,11... | collective-permute-start | bytes 3538952 | tf_op jit(solution)/shard_map/ppermute | solution.py:39
  124.2 43.8 %collective-permute-start.6 = (bf16[1,192,1536]{2,1,0:T(8,128)(2,1)}, bf16[1,192,1536]{2,1,0:T(8,128)(2,1)S(1)}, u32[]{:S(2)}, u32[]{:S(2)}) collective-permute-start(bf16[1,192,1536]{2,1,0:T(8,128)(2,1)} %slice.245), channel_id=1, source_target_pairs={{0,16},{8,24},{16,0},{24,8},{1,17},{9,25},{17,1},{25,9},{2,18},{10... | collective-permute-start | bytes 1769480 | tf_op jit(solution)/shard_map/ppermute | solution.py:39
  130.4 54.2 %collective-permute-start.11 = (bf16[2,768,768]{2,1,0:T(8,128)(2,1)}, bf16[2,768,768]{2,1,0:T(8,128)(2,1)}, u32[]{:S(2)}, u32[]{:S(2)}) collective-permute-start(bf16[2,768,768]{2,1,0:T(8,128)(2,1)} %pad_maximum_fusion.2), channel_id=1, source_target_pairs={{0,2},{2,0},{4,6},{6,4},{1,3},{3,1},{5,7},{7,5},{8,10},{10,8},{12,... | collective-permute-start | bytes 7077896 | tf_op jit(solution)/shard_map/ppermute | solution.py:39
  163.0 27.3 %collective-permute-start.7 = (bf16[1,4,96,1536]{3,2,1,0:T(8,128)(2,1)}, bf16[1,4,96,1536]{3,2,1,0:T(8,128)(2,1)}, u32[]{:S(2)}, u32[]{:S(2)}) collective-permute-start(bf16[1,4,96,1536]{3,2,1,0:T(8,128)(2,1)} %shard_map.105), channel_id=1, source_target_pairs={{0,1},{1,0},{2,3},{3,2},{4,5},{5,4},{6,7},{7,6},{8,9},{9,8},{10,11... | collective-permute-start | bytes 3538952 | tf_op jit(solution)/shard_map/ppermute | solution.py:39
  181.3 33.1 %collective-permute-start.14 = (bf16[1,96,1536]{2,1,0:T(8,128)(2,1)}, bf16[1,96,1536]{2,1,0:T(8,128)(2,1)S(1)}, u32[]{:S(2)}, u32[]{:S(2)}) collective-permute-start(bf16[1,96,1536]{2,1,0:T(8,128)(2,1)} %slice.250), channel_id=1, source_target_pairs={{0,16},{8,24},{16,0},{24,8},{1,17},{9,25},{17,1},{25,9},{2,18},{10... | collective-permute-start | bytes 884744 | tf_op jit(solution)/shard_map/ppermute | solution.py:39
  192.9 32.0 %collective-permute-start.15 = (bf16[2,96,1536]{2,1,0:T(8,128)(2,1)}, bf16[2,96,1536]{2,1,0:T(8,128)(2,1)}, u32[]{:S(2)}, u32[]{:S(2)}) collective-permute-start(bf16[2,96,1536]{2,1,0:T(8,128)(2,1)} %slice.243), channel_id=1, source_target_pairs={{0,8},{8,0},{16,24},{24,16},{1,9},{9,1},{17,25},{25,17},{2,10},{10... | collective-permute-start | bytes 1769480 | tf_op jit(solution)/shard_map/ppermute | solution.py:39
  222.0 22.9 %collective-permute-start.17 = (bf16[1,384,1536]{2,1,0:T(8,128)(2,1)}, bf16[1,384,1536]{2,1,0:T(8,128)(2,1)S(1)}, u32[]{:S(2)}, u32[]{:S(2)}) collective-permute-start(bf16[1,384,1536]{2,1,0:T(8,128)(2,1)} %shard_map.114), channel_id=1, source_target_pairs={{0,1},{1,0},{2,3},{3,2},{4,5},{5,4},{6,7},{7,6},{8,9},{9,8},{10,11... | collective-permute-start | bytes 3538952 | tf_op jit(solution)/shard_map/ppermute | solution.py:39
  248.8 60.5 %all-gather.14.cloned.1.call-start = ((), (), s32[]{:S(2)}) async-start(), calls=%async_computation.2 | async-start | bytes 1474560 | tf_op jit(solution)/shard_map/all_gather | solution.py:470
  252.3 88.6 %all-gather.16.cloned.1.call-start = ((), (), s32[]{:S(2)}) async-start(), calls=%async_computation.3 | async-start | bytes 1474560 | tf_op jit(solution)/shard_map/all_gather | solution.py:470
  252.4 22.2 %collective-permute-start.18 = (bf16[1,384,1536]{2,1,0:T(8,128)(2,1)}, bf16[1,384,1536]{2,1,0:T(8,128)(2,1)}, u32[]{:S(2)}, u32[]{:S(2)}) collective-permute-start(bf16[1,384,1536]{2,1,0:T(8,128)(2,1)} %bitcast.110), channel_id=1, source_target_pairs={{0,1},{1,0},{2,3},{3,2},{4,5},{5,4},{6,7},{7,6},{8,9},{9,8},{10,11... | collective-permute-start | bytes 3538952 | tf_op jit(solution)/shard_map/ppermute | solution.py:39
  257.1 125.0 %all-gather.18.cloned.1.call-start = ((), (), s32[]{:S(2)}) async-start(), calls=%async_computation.4 | async-start | bytes 1474560 | tf_op jit(solution)/shard_map/all_gather | solution.py:470
  278.2 31.2 %collective-permute-start.19 = (bf16[1,4,96,1536]{3,2,1,0:T(8,128)(2,1)}, bf16[1,4,96,1536]{3,2,1,0:T(8,128)(2,1)S(1)}, u32[]{:S(2)}, u32[]{:S(2)}) collective-permute-start(bf16[1,4,96,1536]{3,2,1,0:T(8,128)(2,1)} %shard_map.124.refs_0_), channel_id=1, source_target_pairs={{0,1},{1,0},{2,3},{3,2},{4,5},{5,4},{6,7},{7,6},{8,9},{9,8},{10,11... | collective-permute-start | bytes 3538952 | tf_op jit(solution)/shard_map/ppermute | solution.py:39
  319.2 39.0 %collective-permute-start.20 = (bf16[2,768,768]{2,1,0:T(8,128)(2,1)}, bf16[2,768,768]{2,1,0:T(8,128)(2,1)}, u32[]{:S(2)}, u32[]{:S(2)}) collective-permute-start(bf16[2,768,768]{2,1,0:T(8,128)(2,1)} %shard_map.127), channel_id=1, source_target_pairs={{0,2},{2,0},{4,6},{6,4},{1,3},{3,1},{5,7},{7,5},{8,10},{10,8},{12,... | collective-permute-start | bytes 7077896 | tf_op jit(solution)/shard_map/ppermute | solution.py:39
  319.3 28.6 %collective-permute-start.24 = (bf16[1,4,96,1536]{3,2,1,0:T(8,128)(2,1)}, bf16[1,4,96,1536]{3,2,1,0:T(8,128)(2,1)S(1)}, u32[]{:S(2)}, u32[]{:S(2)}) collective-permute-start(bf16[1,4,96,1536]{3,2,1,0:T(8,128)(2,1)} %shard_map.129.refs_0_.refs_2_), channel_id=1, source_target_pairs={{0,1},{1,0},{2,3},{3,2},{4,5},{5,4},{6,7},{7,6},{8,9},{9,8},{10,11... | collective-permute-start | bytes 3538952 | tf_op jit(solution)/shard_map/ppermute | solution.py:39
  348.9 33.2 %collective-permute-start.25 = (bf16[1,4,96,1536]{3,2,1,0:T(8,128)(2,1)}, bf16[1,4,96,1536]{3,2,1,0:T(8,128)(2,1)S(1)}, u32[]{:S(2)}, u32[]{:S(2)}) collective-permute-start(bf16[1,4,96,1536]{3,2,1,0:T(8,128)(2,1)} %shard_map.131.refs_0_.refs_4_), channel_id=1, source_target_pairs={{0,1},{1,0},{2,3},{3,2},{4,5},{5,4},{6,7},{7,6},{8,9},{9,8},{10,11... | collective-permute-start | bytes 3538952 | tf_op jit(solution)/shard_map/ppermute | solution.py:39
  365.3 43.2 %collective-permute-start.21 = (bf16[1,768,768]{2,1,0:T(8,128)(2,1)}, bf16[1,768,768]{2,1,0:T(8,128)(2,1)}, u32[]{:S(2)}, u32[]{:S(2)}) collective-permute-start(bf16[1,768,768]{2,1,0:T(8,128)(2,1)} %slice.241), channel_id=1, source_target_pairs={{0,4},{2,6},{4,0},{6,2},{1,5},{3,7},{5,1},{7,3},{8,12},{10,14},{12... | collective-permute-start | bytes 3538952 | tf_op jit(solution)/shard_map/ppermute | solution.py:39
  385.6 27.6 %collective-permute-start.26 = (bf16[1,4,96,1536]{3,2,1,0:T(8,128)(2,1)}, bf16[1,4,96,1536]{3,2,1,0:T(8,128)(2,1)}, u32[]{:S(2)}, u32[]{:S(2)}) collective-permute-start(bf16[1,4,96,1536]{3,2,1,0:T(8,128)(2,1)} %shard_map.133.refs_6_), channel_id=1, source_target_pairs={{0,1},{1,0},{2,3},{3,2},{4,5},{5,4},{6,7},{7,6},{8,9},{9,8},{10,11... | collective-permute-start | bytes 3538952 | tf_op jit(solution)/shard_map/ppermute | solution.py:39
  445.1 27.1 %collective-permute-start.29 = (bf16[192,768]{1,0:T(8,128)(2,1)S(1)}, bf16[192,768]{1,0:T(8,128)(2,1)S(1)}, u32[]{:S(2)}, u32[]{:S(2)}) collective-permute-start(bf16[192,768]{1,0:T(8,128)(2,1)S(1)} %fusion.7), channel_id=1, source_target_pairs={{0,0},{2,8},{4,16},{6,24},{8,2},{10,10},{12,18},{14,26},{16,4},{18... | collective-permute-start | bytes 884744 | tf_op jit(solution)/shard_map/ppermute | solution.py:538
  (96 other events, 498.9 us)
Sparse Core Ops, SparseCore 0:
  29.4 18.0 all-gather.9
  248.9 29.1 all-gather.11
  279.7 29.5 all-gather.13
  311.3 29.5 all-gather.15
  342.3 29.5 all-gather.17
